TPU v7x, 128 devices: a whole 4x4x4 slice. The times are simulated.
128 devices in a mesh: clu: 16 (over y, z), smp: 8 (over x, core).
Axes of the slice: x: 4, y: 4, z: 4, core: 2. Of those that a mesh axis runs over, the one named last changes fastest.
Arguments:
- currents: float32 [4096, 2, 128], P(('clu', 'smp')), may hold values from -6 to 6
- near_blocks: bfloat16 [4096, 6, 2, 128, 128], P(('clu', 'smp')), may hold values from -0.15625 to 0.15625
- near_src: int32 [4096, 6], P(('clu', 'smp')), may hold values from 0 to 4095, as said below
- radiation: float32 [2, 128, 256], replicated, may hold values from -0.375 to 0.375
- interp: float32 [256, 1024], replicated, may hold values from -0.375 to 0.375
- shift_phase: float32 [8, 1024], replicated, may hold values from -3.140625 to 3.140625
- parent_map: int32 [16, 256], P('clu'), may hold values from 0 to 95, never falling along the last dimension, each value on 1 to 8 neighbouring positions
- octant: int32 [16, 256], P('clu'), may hold values from 0 to 7
- trans: float32 [316, 2, 1024], P(None, None, 'smp'), may hold values from -0.5 to 0.5
- far_src: int32 [1536, 64], P('clu'), may hold values from 0 to 1535, as said below
- far_kind: int32 [1536, 64], P('clu'), may hold values from 0 to 315, as said below
- receive: float32 [2, 256, 128], replicated, may hold values from -0.125 to 0.125
Outputs:
- product: float32 [4096, 2, 128], P(('clu', 'smp'))
Inputs may be any that keep to these rules, and one draw needn't show every extreme that they name: near_src[l, 0] = l; every entry names a leaf held by the device that holds leaf l or by the device just before or after it in clu+smp order, and both neighbours are named wherever they exist. `parent_map`: numbers never fall along a row; every parent has 1 to 8 children and some parent of each group has exactly 8. `far_src`: the 64 entries of row t are distinct and name parents p with |p // 96 - t // 96| <= 1. far_kind[t, f] = (far_src[t, f] - t) mod 316.
All inputs are finite; a program needn't handle non-finite values.
Results may differ from a plain program's by a relative error of at most 0.0015.
Values may be sent and summed in bfloat16 or wider, within the bound.
A program may use at most 64 MiB of HBM per device.

v0:
```python
import jax
import jax.numpy as jnp
from jax import lax
from jax.sharding import PartitionSpec as P

highest = lax.Precision.HIGHEST


def extended(value, sides, width):
    for axis, dim in sides:
        size, length = (lax.axis_size(axis), value.shape[dim])
        up = [(i, (i + 1) % size) for i in range(size - 1)]
        down = [(j, i) for i, j in up]
        last = lax.slice_in_dim(value, length - width, length, axis=dim)
        first = lax.slice_in_dim(value, 0, width, axis=dim)
        before = lax.ppermute(last, axis, up)
        after = lax.ppermute(first, axis, down)
        value = jnp.concatenate([before, value, after], axis=dim)
    return value


def complex_dot(left_real, left_imag, right_real, right_imag):
    real_part = jnp.dot(
        left_real, right_real, precision=highest, preferred_element_type=jnp.float32
    ) - jnp.dot(left_imag, right_imag, precision=highest, preferred_element_type=jnp.float32)
    imag_part = jnp.dot(
        left_real, right_imag, precision=highest, preferred_element_type=jnp.float32
    ) + jnp.dot(left_imag, right_real, precision=highest, preferred_element_type=jnp.float32)
    return (real_part, imag_part)


def lookup(source_table, indices, entries):
    onehot = (indices[:, None] == jnp.arange(entries, dtype=jnp.int32)[None, :]).astype(jnp.float32)
    return jnp.dot(onehot, source_table, precision=highest, preferred_element_type=jnp.float32)


def collect(onehot, values):
    return jnp.einsum(
        "lp,lk->pk", onehot, values, precision=highest, preferred_element_type=jnp.float32
    )


def near_product(blocks, vectors):
    real_real = jnp.einsum(
        "lsij,lsj->li", blocks[:, :, 0], vectors[:, :, 0], preferred_element_type=jnp.float32
    )
    imag_imag = jnp.einsum(
        "lsij,lsj->li", blocks[:, :, 1], vectors[:, :, 1], preferred_element_type=jnp.float32
    )
    real_imag = jnp.einsum(
        "lsij,lsj->li", blocks[:, :, 0], vectors[:, :, 1], preferred_element_type=jnp.float32
    )
    imag_real = jnp.einsum(
        "lsij,lsj->li", blocks[:, :, 1], vectors[:, :, 0], preferred_element_type=jnp.float32
    )
    return (real_real - imag_imag, real_imag + imag_real)


def translate_all(nearby, source_local, far_kind, trans):
    parents_here = source_local.shape[0]
    slot_count = source_local.shape[1]
    source_total = nearby.shape[0]
    sample_width = nearby.shape[2]
    kind_total = trans.shape[0]
    near_flat = nearby.reshape(source_total, 2 * sample_width)
    ops_flat = trans.reshape(kind_total, 2 * sample_width)
    width_block = 8
    turns = slot_count // width_block
    source_ids = jnp.arange(source_total, dtype=jnp.int32)
    kind_ids = jnp.arange(kind_total, dtype=jnp.int32)

    def accumulate(turn, totals):
        total_real, total_imag = totals
        source_block = lax.dynamic_slice_in_dim(source_local, turn * width_block, width_block, 1)
        kind_block = lax.dynamic_slice_in_dim(far_kind, turn * width_block, width_block, 1)
        source_hot = (source_block[:, :, None] == source_ids[None, None, :]).astype(jnp.float32)
        kind_hot = (kind_block[:, :, None] == kind_ids[None, None, :]).astype(jnp.float32)
        rows = jnp.einsum(
            "pfn,nk->pfk",
            source_hot,
            near_flat,
            precision=highest,
            preferred_element_type=jnp.float32,
        )
        operators = jnp.einsum(
            "pfn,nk->pfk", kind_hot, ops_flat, precision=highest, preferred_element_type=jnp.float32
        )
        rows = rows.reshape(parents_here, width_block, 2, sample_width)
        operators = operators.reshape(parents_here, width_block, 2, sample_width)
        total_real = total_real + jnp.sum(
            operators[:, :, 0] * rows[:, :, 0] - operators[:, :, 1] * rows[:, :, 1], axis=1
        )
        total_imag = total_imag + jnp.sum(
            operators[:, :, 0] * rows[:, :, 1] + operators[:, :, 1] * rows[:, :, 0], axis=1
        )
        return (total_real, total_imag)

    empty = jnp.zeros((parents_here, sample_width), jnp.float32)
    return lax.fori_loop(0, turns, accumulate, (empty, empty))


def on_device(
    currents,
    near_blocks,
    near_src,
    radiation,
    interp,
    shift_phase,
    parent_map,
    octant,
    trans,
    far_src,
    far_kind,
    receive,
):
    leaves_here = currents.shape[0]
    groups = lax.axis_size("smp")
    member = lax.axis_index("smp")
    device = lax.axis_index(("clu", "smp"))
    cluster = lax.axis_index("clu")
    parents_here = far_src.shape[0]
    sample_width = interp.shape[1] // groups
    near_currents = currents.astype(jnp.bfloat16)
    padded = extended(near_currents, ((("clu", "smp"), 0),), leaves_here)
    local_rows = near_src - device * leaves_here + leaves_here
    near_rows = padded[local_rows]
    near_real, near_imag = near_product(near_blocks, near_rows)
    pattern_real, pattern_imag = complex_dot(
        currents[:, 0], currents[:, 1], radiation[0], radiation[1]
    )
    group_parent = parent_map[0]
    group_octant = octant[0]
    own_parent = lax.dynamic_slice_in_dim(group_parent, member * leaves_here, leaves_here)
    own_octant = lax.dynamic_slice_in_dim(group_octant, member * leaves_here, leaves_here)
    cos_table = jnp.cos(shift_phase)
    sin_table = jnp.sin(shift_phase)
    interp_part = lax.dynamic_slice_in_dim(interp, member * sample_width, sample_width, 1)
    cos_part = lax.dynamic_slice_in_dim(cos_table, member * sample_width, sample_width, 1)
    sin_part = lax.dynamic_slice_in_dim(sin_table, member * sample_width, sample_width, 1)
    parent_ids = jnp.arange(parents_here, dtype=jnp.int32)
    inter_real = jnp.dot(
        pattern_real, interp, precision=highest, preferred_element_type=jnp.float32
    )
    inter_imag = jnp.dot(
        pattern_imag, interp, precision=highest, preferred_element_type=jnp.float32
    )
    cos_rows = lookup(cos_table, own_octant, 8)
    sin_rows = lookup(sin_table, own_octant, 8)
    shifted_real = inter_real * cos_rows - inter_imag * sin_rows
    shifted_imag = inter_real * sin_rows + inter_imag * cos_rows
    own_member = (own_parent[:, None] == parent_ids[None, :]).astype(jnp.float32)
    partial_sum = jnp.stack(
        [collect(own_member, shifted_real), collect(own_member, shifted_imag)], axis=1
    )
    upper_pattern = lax.psum_scatter(partial_sum, "smp", scatter_dimension=2, tiled=True)
    nearby = extended(upper_pattern, (("clu", 0),), parents_here)
    source_local = far_src - (cluster - 1) * parents_here
    incoming_real, incoming_imag = translate_all(nearby, source_local, far_kind, trans)
    group_onehot = (group_parent[:, None] == parent_ids[None, :]).astype(jnp.float32)
    parent_real = jnp.dot(
        group_onehot, incoming_real, precision=highest, preferred_element_type=jnp.float32
    )
    parent_imag = jnp.dot(
        group_onehot, incoming_imag, precision=highest, preferred_element_type=jnp.float32
    )
    cos_rows = lookup(cos_part, group_octant, 8)
    sin_rows = lookup(sin_part, group_octant, 8)
    unshift_real = parent_real * cos_rows + parent_imag * sin_rows
    unshift_imag = parent_imag * cos_rows - parent_real * sin_rows
    partial_field = jnp.stack(
        [
            jnp.dot(
                unshift_real, interp_part.T, precision=highest, preferred_element_type=jnp.float32
            ),
            jnp.dot(
                unshift_imag, interp_part.T, precision=highest, preferred_element_type=jnp.float32
            ),
        ],
        axis=1,
    )
    leaf_incoming = lax.psum_scatter(partial_field, "smp", scatter_dimension=0, tiled=True)
    spread_real = leaf_incoming[:, 0]
    spread_imag = leaf_incoming[:, 1]
    far_real, far_imag = complex_dot(spread_real, spread_imag, receive[0], receive[1])
    return jnp.stack([near_real + far_real, near_imag + far_imag], axis=1)


def solution(mesh):
    in_specs = (
        P(("clu", "smp"), None, None),
        P(("clu", "smp"), None, None, None, None),
        P(("clu", "smp"), None),
        P(),
        P(),
        P(),
        P("clu", None),
        P("clu", None),
        P(None, None, "smp"),
        P("clu", None),
        P("clu", None),
        P(),
    )
    out_specs = P(("clu", "smp"), None, None)
    return jax.shard_map(
        on_device, mesh=mesh, in_specs=in_specs, out_specs=out_specs, check_vma=False
    )
```

profile of v0, /device:TPU:0, one launch (start us, length us, event | category | flops | bytes accessed | tf_op | source)
XLA Modules:
  0.0 136.0 jit_solution(12197888589774546928)
XLA Ops:
  6.6 0.9 convert_element_type.8
  7.5 1.3 collective-permute-start
  8.8 1.3 collective-permute-start.1
  10.1 0.9 fusion.86
  10.9 1.1 fusion.34
  12.0 1.1 fusion.30
  13.1 0.9 fusion.85
  14.0 0.8 fusion.82
  15.3 1.1 convolution_subtract_fusion
  16.4 1.1 convolution_add_fusion
  17.5 0.7 fusion.87
  18.2 0.7 fusion.88
  19.8 1.0 pad_maximum_fusion
  22.0 0.8 gather_fusion
  23.0 34.7 %reduce-scatter.3.cloned.1.call-done = f32[96,2,128]{2,0,1:T(8,128)} async-done(((f32[96,2,1024]{2,0,1:T(8,128)}), f32[96,2,128]{2,0,1:T(8,128)}) %reduce-scatter.3.cloned.1.call-update) | async-done | bytes 98320 | tf_op jit(solution)/shard_map/reduce_scatter | solution.py:155
  57.7 3.5 %collective-permute-start.2 = (f32[96,2,128]{2,0,1:T(8,128)}, f32[96,2,128]{2,0,1:T(8,128)S(1)}, u32[]{:S(2)}, u32[]{:S(2)}) collective-permute-start(f32[96,2,128]{2,0,1:T(8,128)} %reduce-scatter.3.cloned.1.call-done), channel_id=1, source_target_pairs={{0,8},{8,16},{16,24},{24,32},{32,40},{40,48},{48,56},{56,64},{64,7... | collective-permute-start | bytes 294920 | tf_op jit(solution)/shard_map/ppermute | solution.py:16
  61.3 1.3 collective-permute-start.3
  62.6 4.5 %fusion.10 = f32[32,1,128,1]{2,1,3,0:T(1,128)S(1)} fusion(bf16[32,6,2,128,128]{4,3,2,1,0:T(8,128)(2,1)} %param.15, bf16[32,6,128,1]{2,0,1,3:T(8,128)(2,1)S(1)} %get-tuple-element.237), kind=kOutput, calls=%fused_computation.19 | convolution fusion | flops 6291456 | bytes 6356992 | tf_op jit(solution)/shard_map/lsij,lsj->li/dot_general | solution.py:47
  67.1 0.9 collective-permute-done.3
  68.0 23.2 %while.16 = (s32[]{:T(128)}, f32[96,128]{1,0:T(8,128)S(1)}, f32[96,128]{1,0:T(8,128)S(1)}, s32[96,64]{0,1:T(8,128)}, f32[316,256]{1,0:T(8,128)S(1)}, /*index=5*/...) while((s32[]{:T(128)}, f32[96,128]{1,0:T(8,128)S(1)}, ...), condition=%wide.region_4.0_spmd.clone, body=%wide.region_1.0_spmd.clone.sunk | while | flops 1426289664 | bytes 4182189 | solution.py:99
  68.0 0.7 constant_dynamic-slice_fusion.7
  68.8 0.8 convolution_bitcast_fusion.9
  69.8 0.9 convolution_bitcast_fusion.8
  70.9 0.7 constant_dynamic-slice_fusion.7
  71.7 0.8 convolution_bitcast_fusion.9
  72.7 0.8 convolution_bitcast_fusion.8
  74.6 0.8 convolution_bitcast_fusion.9
  75.6 0.8 convolution_bitcast_fusion.8
  76.8 0.7 constant_dynamic-slice_fusion.7
  77.5 0.8 convolution_bitcast_fusion.9
  78.5 0.8 convolution_bitcast_fusion.8
  80.5 0.8 convolution_bitcast_fusion.9
  81.4 0.8 convolution_bitcast_fusion.8
  83.4 0.8 convolution_bitcast_fusion.9
  84.3 0.8 convolution_bitcast_fusion.8
  86.3 0.8 convolution_bitcast_fusion.9
  87.2 0.8 convolution_bitcast_fusion.8
  89.2 0.8 convolution_bitcast_fusion.9
  90.1 0.8 convolution_bitcast_fusion.8
  92.6 0.8 pad_maximum_fusion.1
  93.5 4.5 %fusion.12 = f32[32,1,128,1]{2,1,3,0:T(1,128)S(1)} fusion(bf16[32,6,2,128,128]{4,3,2,1,0:T(8,128)(2,1)} %param.15, bf16[32,6,128,1]{2,0,1,3:T(8,128)(2,1)S(1)} %get-tuple-element.237), kind=kOutput, calls=%fused_computation.21 | convolution fusion | flops 6291456 | bytes 6356992 | tf_op jit(solution)/shard_map/lsij,lsj->li/dot_general | solution.py:50
  98.0 4.6 %fusion.14 = f32[32,1,128,1]{2,1,3,0:T(1,128)S(1)} fusion(bf16[32,6,2,128,128]{4,3,2,1,0:T(8,128)(2,1)} %param.15, bf16[32,6,128,1]{2,0,1,3:T(8,128)(2,1)S(1)} %get-tuple-element.238), kind=kOutput, calls=%fused_computation.23 | convolution fusion | flops 6291456 | bytes 6356992 | tf_op jit(solution)/shard_map/lsij,lsj->li/dot_general | solution.py:44
  102.6 4.6 %fusion.8 = f32[32,1,128,1]{2,1,3,0:T(1,128)S(1)} fusion(bf16[32,6,2,128,128]{4,3,2,1,0:T(8,128)(2,1)} %param.15, bf16[32,6,128,1]{2,0,1,3:T(8,128)(2,1)S(1)} %get-tuple-element.238), kind=kOutput, calls=%fused_computation.17 | convolution fusion | flops 6291456 | bytes 6356992 | tf_op jit(solution)/shard_map/lsij,lsj->li/dot_general | solution.py:53
  107.1 17.6 %reduce-scatter.5.cloned.1.call-done = f32[32,2,256]{2,0,1:T(8,128)} async-done(((f32[256,2,256]{2,0,1:T(8,128)}), f32[32,2,256]{2,0,1:T(8,128)}) %reduce-scatter.5.cloned.1.call-update) | async-done | bytes 65552 | tf_op jit(solution)/shard_map/reduce_scatter | solution.py:181
  124.7 0.9 fusion.28
  125.7 0.9 fusion.24
  126.6 1.0 fusion.23
  127.6 1.0 fusion.21
  (86 shorter events, 11.8 us)
Async XLA Ops:
  6.5 10.9 %copy-start = (f32[256,1024]{1,0:T(8,128)S(1)}, f32[256,1024]{1,0:T(8,128)}, u32[]{:S(2)}) copy-start(f32[256,1024]{1,0:T(8,128)} %param.18) | copy-start | bytes 3145732
  6.5 14.6 %copy-start.5 = (s32[1,256]{1,0:T(1,128)S(1)}, s32[1,256]{1,0:T(1,128)}, u32[]{:S(2)}) copy-start(s32[1,256]{1,0:T(1,128)} %param.21) | copy-start | bytes 3076
  6.5 14.3 %copy-start.4 = (s32[96,64]{0,1:T(8,128)S(1)}, s32[96,64]{0,1:T(8,128)}, u32[]{:S(2)}) copy-start(s32[96,64]{0,1:T(8,128)} %param.23) | copy-start | bytes 73732
  6.5 14.4 %copy-start.7 = (s32[32,6]{0,1:T(8,128)S(1)}, s32[32,6]{0,1:T(8,128)}, u32[]{:S(2)}) copy-start(s32[32,6]{0,1:T(8,128)} %param.16) | copy-start | bytes 2308
  6.5 15.2 %copy-start.2 = (f32[316,2,128]{2,1,0:T(2,128)S(1)}, f32[316,2,128]{2,1,0:T(2,128)}, u32[]{:S(2)}) copy-start(f32[316,2,128]{2,1,0:T(2,128)} %param.22) | copy-start | bytes 970756
  6.5 51.2 %reduce-scatter.3.cloned.1.call-start = ((), (), s32[]{:S(2)}) async-start(), calls=%async_computation.2 | async-start | bytes 884736 | tf_op jit(solution)/shard_map/reduce_scatter | solution.py:155
  7.5 14.4 %collective-permute-start = (bf16[32,2,128]{2,1,0:T(2,128)(2,1)S(1)}, bf16[32,2,128]{2,1,0:T(2,128)(2,1)S(1)}, u32[]{:S(2)}, u32[]{:S(2)}) collective-permute-start(bf16[32,2,128]{2,1,0:T(2,128)(2,1)S(1)} %convert_element_type.8), channel_id=1, source_target_pairs={{0,1},{1,2},{2,3},{3,4},{4,5},{5,6},{6,7},{7,8},{8,9},{9,10},{10,1... | collective-permute-start | bytes 49160 | tf_op jit(solution)/shard_map/ppermute | solution.py:16
  8.8 13.1 %collective-permute-start.1 = (bf16[32,2,128]{2,1,0:T(2,128)(2,1)S(1)}, bf16[32,2,128]{2,1,0:T(2,128)(2,1)S(1)}, u32[]{:S(2)}, u32[]{:S(2)}) collective-permute-start(bf16[32,2,128]{2,1,0:T(2,128)(2,1)S(1)} %convert_element_type.8), channel_id=1, source_target_pairs={{1,0},{2,1},{3,2},{4,3},{5,4},{6,5},{7,6},{8,7},{9,8},{10,9},{11,1... | collective-permute-start | bytes 49160 | tf_op jit(solution)/shard_map/ppermute | solution.py:17
  20.8 103.9 %reduce-scatter.5.cloned.1.call-start = ((), (), s32[]{:S(2)}) async-start(), calls=%async_computation.3 | async-start | bytes 589824 | tf_op jit(solution)/shard_map/reduce_scatter | solution.py:181
  57.7 10.2 %copy-start.3 = (f32[96,2,128]{2,0,1:T(8,128)S(1)}, f32[96,2,128]{2,0,1:T(8,128)}, u32[]{:S(2)}) copy-start(f32[96,2,128]{2,0,1:T(8,128)} %reduce-scatter.3.cloned.1.call-done) | copy-start | bytes 294916
  57.7 9.4 %collective-permute-start.2 = (f32[96,2,128]{2,0,1:T(8,128)}, f32[96,2,128]{2,0,1:T(8,128)S(1)}, u32[]{:S(2)}, u32[]{:S(2)}) collective-permute-start(f32[96,2,128]{2,0,1:T(8,128)} %reduce-scatter.3.cloned.1.call-done), channel_id=1, source_target_pairs={{0,8},{8,16},{16,24},{24,32},{32,40},{40,48},{48,56},{56,64},{64,7... | collective-permute-start | bytes 294920 | tf_op jit(solution)/shard_map/ppermute | solution.py:16
  61.3 6.7 %collective-permute-start.3 = (f32[96,2,128]{2,0,1:T(8,128)}, f32[96,2,128]{2,0,1:T(8,128)S(1)}, u32[]{:S(2)}, u32[]{:S(2)}) collective-permute-start(f32[96,2,128]{2,0,1:T(8,128)} %reduce-scatter.3.cloned.1.call-done), channel_id=1, source_target_pairs={{8,0},{16,8},{24,16},{32,24},{40,32},{48,40},{56,48},{64,56},{72,6... | collective-permute-start | bytes 294920 | tf_op jit(solution)/shard_map/ppermute | solution.py:17
  68.0 23.3 %copy-start.6 = (s32[1,256]{1,0:T(1,128)S(1)}, s32[1,256]{1,0:T(1,128)}, u32[]{:S(2)}) copy-start(s32[1,256]{1,0:T(1,128)} %param.20) | copy-start | bytes 3076
  98.0 26.7 %copy-start.1 = (f32[2,256,128]{2,1,0:T(8,128)S(1)}, f32[2,256,128]{2,1,0:T(8,128)}, u32[]{:S(2)}) copy-start(f32[2,256,128]{2,1,0:T(8,128)} %param.25) | copy-start | bytes 786436
Sparse Core Ops, SparseCore 0:
  20.9 36.8 reduce-scatter.2
  93.6 31.0 reduce-scatter.4
where the time goes:
time: 137 us; the launch traced here: 136 us
  waiting for transfers between devices  53.2 us (39%)
  matrix products  44.4 us (32%)
  between operations  13.8 us (10%)
  local copies, waits for them, and re-layouts  11.5 us (8%)
  starting transfers between devices  7.47 us (5%)
  other arithmetic  5.11 us (4%)
    reduce_scatter x1, waiting for transfers between devices, on_device(): lax.psum_scatter(partial_sum, 'smp', scatter_dimension=2, tiled=True)  34.7 us
    reduce_scatter x1, waiting for transfers between devices, on_device(): lax.psum_scatter(partial_field, 'smp', scatter_dimension=0, tiled=True)  17.6 us
    dot_general x8, matrix products, accumulate(): jnp.einsum('pfn,nk->pfk', source_hot, near_flat, precision=highest, prefe...  6.79 us
    dot_general x8, matrix products, accumulate(): jnp.einsum('pfn,nk->pfk', kind_hot, ops_flat, precision=highest, preferre...  6.74 us
    dynamic_slice x16, local copies, waits for them, and re-layouts, accumulate(): lax.dynamic_slice_in_dim(far_kind, turn * width_block, width_block, 1)  6.3 us
    ppermute x2, starting transfers between devices, extended(): before = lax.ppermute(last, axis, up)  4.81 us
    dot_general x1, matrix products, near_product(): jnp.einsum('lsij,lsj->li', blocks[:, :, 0], vectors[:, :, 0], preferred_e...  4.59 us
    dot_general x1, matrix products, near_product(): jnp.einsum('lsij,lsj->li', blocks[:, :, 1], vectors[:, :, 0], preferred_e...  4.55 us
  transfers between devices with their start and end apart: 6, of which 3 were waited for; matrix products, arithmetic and copies ran while one was open for 23% of the time, Pallas kernels for 0%

commit v1 on v0

v1 whole, which is shorter than its diff:
```python
import functools

import jax
import jax.numpy as jnp
from jax import lax
from jax.experimental import pallas as pl
from jax.experimental.pallas import tpu as pltpu
from jax.sharding import PartitionSpec as P

MESH = pl.DeviceIdType.MESH
F32 = jnp.float32
BF16 = jnp.bfloat16
I32 = jnp.int32
HIGHEST = lax.Precision.HIGHEST
NN = (((1,), (0,)), ((), ()))
NT = (((1,), (1,)), ((), ()))
TN = (((0,), (0,)), ((), ()))

CLU = 16
SMP = 8
LEAF = 32
GROUP = 256
PAR = 96
SLOTS = 6
KINDS = 316
TABLE = 384
BLOCKS = PAR // 8
WORDS = 9
CHUNK = 8
CHUNKS = LEAF // CHUNK
ORDER = (4, 3, 5, 2, 6, 1, 7)


def iota(shape, axis):
    return lax.broadcasted_iota(I32, shape, axis)


def mm(left, right, dims=NN, precision=None):
    return lax.dot_general(left, right, dims, precision=precision, preferred_element_type=F32)


def halves(value):
    high = value.astype(BF16)
    return high, (value - high.astype(F32)).astype(BF16)


def stacked(value):
    high, low = halves(value)
    return jnp.concatenate([high, low, high], axis=0)


def split3(value):
    high, low = halves(value)
    return jnp.concatenate([high, high, low], axis=1)


def complex_square(real, imag):
    return jnp.concatenate(
        [jnp.concatenate([real, imag], axis=1), jnp.concatenate([-imag, real], axis=1)], axis=0
    )


def far_masks(source):
    bits = jnp.left_shift(jnp.ones_like(source), source & 7).astype(F32)
    octet = lax.shift_right_logical(source, jnp.full_like(source, 3))
    rows = iota((40, PAR), 0)
    table = jnp.zeros((40, PAR), F32)
    for f in range(64):
        table = table + jnp.where(octet[f : f + 1] == rows, bits[f : f + 1], 0.0)
    flip = ((iota((PAR, PAR), 0) ^ 7) == iota((PAR, PAR), 1)).astype(BF16)
    table = jnp.concatenate([table, jnp.zeros((88, PAR), F32)], axis=0)
    octets = mm(flip, table.astype(BF16), NT).astype(I32)
    octets = jnp.left_shift(octets, 8 * (iota((PAR, 128), 1) & 3))
    pairs = octets + pltpu.roll(octets, 127, axis=1)
    return pairs + pltpu.roll(pairs, 126, axis=1)


def body(
    cur,
    blocks,
    near_src,
    rad,
    itp,
    phase,
    pmap,
    octant,
    trans,
    far_src,
    rec,
    out,
    xall,
    near_cur,
    near_blk,
    ns_v,
    rad_v,
    itp_v,
    ph_v,
    pm_v,
    oc_v,
    tr_v,
    fs_v,
    rec_v,
    t_re,
    t_im,
    upper,
    m_op,
    n_op,
    shift,
    to_parent,
    to_leaf,
    words,
    near_x,
    near_acc,
    part,
    arrived,
    load_sem,
    blk_sem,
    near_send,
    near_recv,
    cur_send,
    cur_recv,
    up_send,
    up_recv,
    part_send,
    part_recv,
):
    clu = lax.axis_index("clu")
    me = lax.axis_index("smp")
    device = clu * SMP + me
    after = lax.rem(device + 1, CLU * SMP)
    before = lax.rem(device + CLU * SMP - 1, CLU * SMP)
    after_id = (after // SMP, lax.rem(after, SMP))
    before_id = (before // SMP, lax.rem(before, SMP))
    up_id = (lax.rem(clu + 1, CLU), me)
    down_id = (lax.rem(clu + CLU - 1, CLU), me)
    peers = {o: (clu, lax.rem(me + o, SMP)) for o in range(1, SMP)}

    barrier = pltpu.get_barrier_semaphore()
    for where in (after_id, before_id, up_id, down_id, *peers.values()):
        pl.semaphore_signal(barrier, inc=1, device_id=where, device_id_type=MESH)

    columns = pl.ds(pl.multiple_of(me * 128, 128), 128)
    loads = [
        (cur, xall.at[me]),
        (itp.at[:, columns], itp_v),
        (phase.at[:, columns], ph_v),
        (rad, rad_v),
        (rec, rec_v),
        (pmap, pm_v),
        (octant, oc_v),
        (far_src, fs_v),
        (near_src, ns_v),
        (trans.at[pl.ds(KINDS - 192, 192)], tr_v.at[pl.ds(0, 192)]),
        (trans.at[pl.ds(0, 192)], tr_v.at[pl.ds(192, 192)]),
    ]
    copies = [
        pltpu.make_async_copy(source, target, load_sem.at[i])
        for i, (source, target) in enumerate(loads)
    ]
    for copy in copies:
        copy.start()
    blk_copies = [
        pltpu.make_async_copy(
            blocks.at[pl.ds(i * CHUNK, CHUNK)], near_blk.at[pl.ds(i * CHUNK, CHUNK)], blk_sem.at[i]
        )
        for i in range(CHUNKS)
    ]
    for copy in blk_copies:
        copy.start()

    copies[0].wait()
    near_cur[1, 0] = xall[me, :, 0, :].astype(BF16)
    near_cur[1, 1] = xall[me, :, 1, :].astype(BF16)

    pl.semaphore_wait(barrier, 4 + SMP - 1)
    near_out = [
        pltpu.make_async_remote_copy(
            src_ref=near_cur.at[1],
            dst_ref=near_cur.at[slot],
            send_sem=near_send.at[i],
            recv_sem=near_recv.at[i],
            device_id=where,
            device_id_type=MESH,
        )
        for i, (slot, where) in enumerate(((0, after_id), (2, before_id)))
    ]
    for copy in near_out:
        copy.start()
    cur_out = [
        pltpu.make_async_remote_copy(
            src_ref=xall.at[me],
            dst_ref=xall.at[me],
            send_sem=cur_send.at[o - 1],
            recv_sem=cur_recv.at[o - 1],
            device_id=peers[o],
            device_id_type=MESH,
        )
        for o in ORDER
    ]
    for copy in cur_out:
        copy.start()

    for copy in copies[1:9]:
        copy.wait()
    grid = itp_v[...]
    both = mm(rad_v[...].reshape(256, 256), grid, NN, HIGHEST)
    m_op[...] = stacked(complex_square(both[:128], both[128:]))
    both = mm(grid, jnp.concatenate([rec_v[0], rec_v[1]], axis=1), TN, HIGHEST)
    n_op[...] = stacked(complex_square(both[:, :128], both[:, 128:]))
    angles = ph_v[...]
    table = jnp.concatenate([jnp.cos(angles), jnp.sin(angles)], axis=1)
    position = (oc_v[...] == iota((8, GROUP), 0)).astype(F32)
    shift[...] = mm(position, table, TN, HIGHEST)
    owner = pm_v[...]
    member = (owner == iota((PAR, GROUP), 0)).astype(BF16)
    to_parent[...] = jnp.concatenate([member, member], axis=1)
    member = (owner == (iota((PAR, GROUP), 0) ^ 7)).astype(F32)
    to_leaf[...] = jnp.concatenate([member, member], axis=0).T.astype(BF16)
    masks = far_masks(fs_v[...] - (clu - 1) * PAR)
    for q in range(WORDS):
        words[q] = jnp.broadcast_to(masks[:, 4 * q : 4 * q + 1], (PAR, 128))
    copies[9].wait()
    copies[10].wait()
    t_re[...] = tr_v[:, 0, :]
    t_im[...] = tr_v[:, 1, :]

    for copy in near_out:
        copy.wait_recv()
    p_re = near_cur[:, 0].reshape(PAR, 128).astype(F32)
    p_im = near_cur[:, 1].reshape(PAR, 128).astype(F32)
    sources = jnp.concatenate(
        [jnp.concatenate([p_re, -p_im], axis=1), jnp.concatenate([p_im, p_re], axis=1)], axis=0
    )
    local = ns_v[...] - (device - 1) * LEAF
    local = jnp.concatenate(
        [local, local + PAR, jnp.full((SLOTS, 64), -1, I32)], axis=1
    )
    rows = iota((2 * PAR, 128), 0)
    picks = jnp.concatenate(
        [(local[s : s + 1] == rows).astype(F32) for s in range(SLOTS)], axis=1
    ).astype(BF16)
    rhs = mm(sources.T.astype(BF16), picks).astype(BF16)
    for s in range(SLOTS):
        near_x[pl.ds(s * 256, 256)] = rhs[:, s * 128 : (s + 1) * 128]

    lane_leaf = lax.rem(iota((128, 128), 1), LEAF)

    def near_chunk(i):
        blk_copies[i].wait()
        total = near_acc[...] if i else jnp.zeros((128, 128), F32)
        lhs = jnp.concatenate(
            [
                near_blk[pl.ds(i * CHUNK, CHUNK), s, c].reshape(CHUNK * 128, 128)
                for s in range(SLOTS)
                for c in range(2)
            ],
            axis=1,
        )
        result = mm(lhs, near_x[...])
        for r in range(CHUNK):
            total = jnp.where(
                lane_leaf == i * CHUNK + r, result[r * 128 : (r + 1) * 128], total
            )
        near_acc[...] = total

    for copy in cur_out:
        copy.wait_recv()
    x = jnp.concatenate(
        [xall[:, :, 0, :].reshape(GROUP, 128), xall[:, :, 1, :].reshape(GROUP, 128)], axis=1
    )
    inter = mm(split3(x), m_op[...])
    cos, sin = shift[:, :128], shift[:, 128:]
    real, imag = inter[:, :128], inter[:, 128:]
    shifted = jnp.concatenate([real * cos - imag * sin, real * sin + imag * cos], axis=1)
    own = mm(to_parent[...], jnp.concatenate(halves(shifted), axis=0))
    upper[1, 0] = own[:, :128]
    upper[1, 1] = own[:, 128:]
    up_out = [
        pltpu.make_async_remote_copy(
            src_ref=upper.at[1],
            dst_ref=upper.at[slot],
            send_sem=up_send.at[i],
            recv_sem=up_recv.at[i],
            device_id=where,
            device_id_type=MESH,
        )
        for i, (slot, where) in enumerate(((0, up_id), (2, down_id)))
    ]
    for copy in up_out:
        copy.start()

    def translate(group, sums):
        def word_step(turn, sums):
            word = 3 * group + turn

            def octet_step(step, sums):
                sums = list(sums)
                start = pl.multiple_of(32 * turn + 8 * step, 8)
                up_re = upper[group, 0, pl.ds(start, 8)]
                up_im = upper[group, 1, pl.ds(start, 8)]
                offset = jnp.full((8, 128), 8 * step, I32)
                marks = [
                    lax.shift_right_logical(words[word, 8 * b : 8 * b + 8], offset)
                    for b in range(BLOCKS)
                ]
                for i in range(8):
                    source_re = jnp.broadcast_to(up_re[i : i + 1], (8, 128))
                    source_im = jnp.broadcast_to(up_im[i : i + 1], (8, 128))
                    for b in range(BLOCKS):
                        at = 96 * group + start + (89 + i - 8 * b)
                        op_re = t_re[pl.ds(at, 8)]
                        op_im = t_im[pl.ds(at, 8)]
                        there = (marks[b] & (1 << i)) != 0
                        here_re = jnp.where(there, source_re, 0.0)
                        here_im = jnp.where(there, source_im, 0.0)
                        sums[2 * b] = sums[2 * b] + (op_re * here_re - op_im * here_im)
                        sums[2 * b + 1] = sums[2 * b + 1] + (op_re * here_im + op_im * here_re)
                return tuple(sums)

            return lax.fori_loop(0, 4, octet_step, sums)

        return lax.fori_loop(0, 3, word_step, sums)

    sums = tuple(jnp.zeros((8, 128), F32) for _ in range(2 * BLOCKS))
    sums = translate(1, sums)
    near_chunk(0)
    up_out[0].wait_recv()
    sums = translate(0, sums)
    up_out[1].wait_recv()
    sums = translate(2, sums)

    incoming = jnp.concatenate(
        [jnp.concatenate(sums[0::2], axis=0), jnp.concatenate(sums[1::2], axis=0)], axis=1
    )
    field = mm(to_leaf[...], jnp.concatenate(halves(incoming), axis=0))
    cos, sin = shift[:, :128], shift[:, 128:]
    real, imag = field[:, :128], field[:, 128:]
    back = jnp.concatenate([real * cos + imag * sin, imag * cos - real * sin], axis=1)
    part[...] = mm(split3(back), n_op[...]).reshape(SMP, LEAF, 256)
    part_out = [
        pltpu.make_async_remote_copy(
            src_ref=part.at[lax.rem(me + o, SMP)],
            dst_ref=arrived.at[o - 1],
            send_sem=part_send.at[o - 1],
            recv_sem=part_recv.at[o - 1],
            device_id=peers[o],
            device_id_type=MESH,
        )
        for o in ORDER
    ]
    for copy in part_out:
        copy.start()
    for i in range(1, CHUNKS):
        near_chunk(i)
    near = near_acc[...].T
    total = part[me] + jnp.concatenate([near[:LEAF], near[LEAF : 2 * LEAF]], axis=1)
    for copy, o in zip(part_out, ORDER):
        copy.wait_recv()
        total = total + arrived[o - 1]
    out[:, 0, :] = total[:, :128]
    out[:, 1, :] = total[:, 128:]
    for copy in (*near_out, *cur_out, *up_out, *part_out):
        copy.wait_send()


def on_device(
    currents,
    near_blocks,
    near_src,
    radiation,
    interp,
    shift_phase,
    parent_map,
    octant,
    trans,
    far_src,
    far_kind,
    receive,
):
    hbm_spec = pl.BlockSpec(memory_space=pltpu.HBM)
    vmem = pltpu.VMEM
    dma = pltpu.SemaphoreType.DMA
    return pl.pallas_call(
        body,
        out_shape=jax.ShapeDtypeStruct((LEAF, 2, 128), F32),
        in_specs=[hbm_spec] * 11,
        out_specs=pl.BlockSpec(memory_space=vmem),
        scratch_shapes=[
            vmem((SMP, LEAF, 2, 128), F32),
            vmem((3, 2, LEAF, 128), BF16),
            vmem((LEAF, SLOTS, 2, 128, 128), BF16),
            vmem((SLOTS, LEAF), I32),
            vmem((2, 128, 256), F32),
            vmem((256, 128), F32),
            vmem((8, 128), F32),
            vmem((1, GROUP), I32),
            vmem((1, GROUP), I32),
            vmem((TABLE, 2, 128), F32),
            vmem((64, PAR), I32),
            vmem((2, 256, 128), F32),
            vmem((TABLE, 128), F32),
            vmem((TABLE, 128), F32),
            vmem((3, 2, PAR, 128), F32),
            vmem((768, 256), BF16),
            vmem((768, 256), BF16),
            vmem((GROUP, 256), F32),
            vmem((PAR, 512), BF16),
            vmem((GROUP, 192), BF16),
            vmem((WORDS, PAR, 128), I32),
            vmem((SLOTS * 256, 128), BF16),
            vmem((128, 128), F32),
            vmem((SMP, LEAF, 256), F32),
            vmem((SMP - 1, LEAF, 256), F32),
            dma((11,)),
            dma((CHUNKS,)),
            dma((2,)),
            dma((2,)),
            dma((SMP - 1,)),
            dma((SMP - 1,)),
            dma((2,)),
            dma((2,)),
            dma((SMP - 1,)),
            dma((SMP - 1,)),
        ],
        compiler_params=pltpu.CompilerParams(
            collective_id=0, has_side_effects=True, vmem_limit_bytes=48 * 1024 * 1024
        ),
        name="far_and_near",
    )(
        currents,
        near_blocks,
        near_src.T,
        radiation,
        interp,
        shift_phase,
        parent_map,
        octant,
        trans,
        far_src.T,
        receive,
    )


def solution(mesh):
    in_specs = (
        P(("clu", "smp"), None, None),
        P(("clu", "smp"), None, None, None, None),
        P(("clu", "smp"), None),
        P(),
        P(),
        P(),
        P("clu", None),
        P("clu", None),
        P(None, None, "smp"),
        P("clu", None),
        P("clu", None),
        P(),
    )
    out_specs = P(("clu", "smp"), None, None)
    return jax.shard_map(
        on_device, mesh=mesh, in_specs=in_specs, out_specs=out_specs, check_vma=False
    )
```

time: 137 us -> 38.8 us (0.28)
  the two profiles are of different devices: /device:TPU:0 before, /device:TPU:1 now
where the time goes in v1:
time: 38.8 us; the launch traced here: 38.3 us
  Pallas kernels  29.3 us (76%)
  local copies, waits for them, and re-layouts  9.03 us (23%)
    pallas_call x1, Pallas kernels, on_device(): pl.pallas_call(body, out_shape=jax.ShapeDtypeStruct((LEAF, 2, 128), F32),...  29.3 us
    unnamed x21, local copies, waits for them, and re-layouts  9.03 us

profile of v1, /device:TPU:1, one launch (start us, length us, event | category | flops | bytes accessed | tf_op | source)
XLA Modules:
  0.0 38.3 jit_solution(15520818658518624684)
XLA Ops:
  0.0 0.0 copy-start
  0.0 1.2 %copy-done = f32[256,1024]{1,0:T(8,128)S(1)} copy-done((f32[256,1024]{1,0:T(8,128)S(1)}, f32[256,1024]{1,0:T(8,128)}, u32[]{:S(2)}) %copy-start) | copy-done | bytes 1048600
  1.2 0.0 copy-start.1
  1.2 1.0 %copy-done.1 = f32[316,2,128]{2,1,0:T(2,128)S(1)} copy-done((f32[316,2,128]{2,1,0:T(2,128)S(1)}, f32[316,2,128]{2,1,0:T(2,128)}, u32[]{:S(2)}) %copy-start.1) | copy-done | bytes 323608
  2.2 0.0 copy-start.2
  2.2 0.9 %copy-done.2 = f32[2,128,256]{2,1,0:T(8,128)S(1)} copy-done((f32[2,128,256]{2,1,0:T(8,128)S(1)}, f32[2,128,256]{2,1,0:T(8,128)}, u32[]{:S(2)}) %copy-start.2) | copy-done | bytes 262168
  3.1 0.0 copy-start.3
  3.2 0.9 %copy-done.3 = f32[2,256,128]{2,1,0:T(8,128)S(1)} copy-done((f32[2,256,128]{2,1,0:T(8,128)S(1)}, f32[2,256,128]{2,1,0:T(8,128)}, u32[]{:S(2)}) %copy-start.3) | copy-done | bytes 262168
  4.1 0.0 copy-start.4
  4.1 0.8 %copy-done.4 = f32[32,2,128]{2,1,0:T(2,128)S(1)} copy-done((f32[32,2,128]{2,1,0:T(2,128)S(1)}, f32[32,2,128]{2,1,0:T(2,128)}, u32[]{:S(2)}) %copy-start.4) | copy-done | bytes 32792
  4.9 0.0 copy-start.5
  4.9 0.8 %copy-done.5 = f32[8,1024]{1,0:T(8,128)S(1)} copy-done((f32[8,1024]{1,0:T(8,128)S(1)}, f32[8,1024]{1,0:T(8,128)}, u32[]{:S(2)}) %copy-start.5) | copy-done | bytes 32792
  5.6 0.0 copy-start.6
  5.6 0.8 %copy-done.6 = s32[96,64]{0,1:T(8,128)S(1)} copy-done((s32[96,64]{0,1:T(8,128)S(1)}, s32[96,64]{0,1:T(8,128)}, u32[]{:S(2)}) %copy-start.6) | copy-done | bytes 24600
  6.4 0.0 copy-start.7
  6.4 0.7 %copy-done.7 = s32[32,6]{0,1:T(8,128)S(1)} copy-done((s32[32,6]{0,1:T(8,128)S(1)}, s32[32,6]{0,1:T(8,128)}, u32[]{:S(2)}) %copy-start.7) | copy-done | bytes 792
  7.1 0.0 copy-start.8
  7.1 0.7 %copy-done.8 = s32[1,256]{1,0:T(1,128)S(1)} copy-done((s32[1,256]{1,0:T(1,128)S(1)}, s32[1,256]{1,0:T(1,128)}, u32[]{:S(2)}) %copy-start.8) | copy-done | bytes 1048
  7.7 0.0 copy-start.9
  7.7 0.7 %copy-done.9 = s32[1,256]{1,0:T(1,128)S(1)} copy-done((s32[1,256]{1,0:T(1,128)S(1)}, s32[1,256]{1,0:T(1,128)}, u32[]{:S(2)}) %copy-start.9) | copy-done | bytes 1048
  8.4 29.3 %far_and_near.1 = f32[32,2,128]{2,1,0:T(2,128)S(1)} custom-call(f32[32,2,128]{2,1,0:T(2,128)S(1)} %copy-done.4, bf16[32,6,2,128,128]{4,3,2,1,0:T(8,128)(2,1)} %blocks.1, s32[6,32]{1,0:T(8,128)S(1)} %bitcast.3, f32[2,128,256]{2,1,0:T(8,128)S(1)} %copy-done.2, f32[256,1024]{1,0:T(8,128)S(1)} %copy-done, f32[8,1024]{1,0:T(8,128)S(1)} %copy-done.5, ...), custom_call_target="tpu_custom_call" | custom-call | tf_op jit(solution)/shard_map/far_and_near/pallas_call | solution.py:383
  37.7 0.6 %copy.13 = f32[32,2,128]{2,1,0:T(2,128)} copy(f32[32,2,128]{2,1,0:T(2,128)S(1)} %far_and_near.1) | data formatting | bytes 65536
Async XLA Ops:
  0.0 1.2 %copy-start = (f32[256,1024]{1,0:T(8,128)S(1)}, f32[256,1024]{1,0:T(8,128)}, u32[]{:S(2)}) copy-start(f32[256,1024]{1,0:T(8,128)} %itp.1) | copy-start | bytes 3145732
  1.2 1.0 %copy-start.1 = (f32[316,2,128]{2,1,0:T(2,128)S(1)}, f32[316,2,128]{2,1,0:T(2,128)}, u32[]{:S(2)}) copy-start(f32[316,2,128]{2,1,0:T(2,128)} %trans.1) | copy-start | bytes 970756
  2.2 0.9 %copy-start.2 = (f32[2,128,256]{2,1,0:T(8,128)S(1)}, f32[2,128,256]{2,1,0:T(8,128)}, u32[]{:S(2)}) copy-start(f32[2,128,256]{2,1,0:T(8,128)} %rad.1) | copy-start | bytes 786436
  3.1 0.9 %copy-start.3 = (f32[2,256,128]{2,1,0:T(8,128)S(1)}, f32[2,256,128]{2,1,0:T(8,128)}, u32[]{:S(2)}) copy-start(f32[2,256,128]{2,1,0:T(8,128)} %rec.1) | copy-start | bytes 786436
  4.1 0.8 %copy-start.4 = (f32[32,2,128]{2,1,0:T(2,128)S(1)}, f32[32,2,128]{2,1,0:T(2,128)}, u32[]{:S(2)}) copy-start(f32[32,2,128]{2,1,0:T(2,128)} %cur.1) | copy-start | bytes 98308
  4.9 0.8 %copy-start.5 = (f32[8,1024]{1,0:T(8,128)S(1)}, f32[8,1024]{1,0:T(8,128)}, u32[]{:S(2)}) copy-start(f32[8,1024]{1,0:T(8,128)} %phase.1) | copy-start | bytes 98308
  5.6 0.8 %copy-start.6 = (s32[96,64]{0,1:T(8,128)S(1)}, s32[96,64]{0,1:T(8,128)}, u32[]{:S(2)}) copy-start(s32[96,64]{0,1:T(8,128)} %param.21) | copy-start | bytes 73732
  6.4 0.7 %copy-start.7 = (s32[32,6]{0,1:T(8,128)S(1)}, s32[32,6]{0,1:T(8,128)}, u32[]{:S(2)}) copy-start(s32[32,6]{0,1:T(8,128)} %param.14) | copy-start | bytes 2308
  7.1 0.7 %copy-start.8 = (s32[1,256]{1,0:T(1,128)S(1)}, s32[1,256]{1,0:T(1,128)}, u32[]{:S(2)}) copy-start(s32[1,256]{1,0:T(1,128)} %pmap.1) | copy-start | bytes 3076
  7.7 0.7 %copy-start.9 = (s32[1,256]{1,0:T(1,128)S(1)}, s32[1,256]{1,0:T(1,128)}, u32[]{:S(2)}) copy-start(s32[1,256]{1,0:T(1,128)} %octant.1) | copy-start | bytes 3076

commit v2 on v1

--- a/solution.py
+++ b/solution.py
@@ -111,6 +111,7 @@
     words,
     near_x,
     near_acc,
+    incoming,
     part,
     arrived,
     load_sem,
@@ -127,17 +128,32 @@
     clu = lax.axis_index("clu")
     me = lax.axis_index("smp")
     device = clu * SMP + me
-    after = lax.rem(device + 1, CLU * SMP)
-    before = lax.rem(device + CLU * SMP - 1, CLU * SMP)
-    after_id = (after // SMP, lax.rem(after, SMP))
-    before_id = (before // SMP, lax.rem(before, SMP))
+    after = device + 1
+    before = device + CLU * SMP - 1
+    after_id = (lax.rem(after // SMP, CLU), lax.rem(after, SMP))
+    before_id = (lax.rem(before // SMP, CLU), lax.rem(before, SMP))
     up_id = (lax.rem(clu + 1, CLU), me)
     down_id = (lax.rem(clu + CLU - 1, CLU), me)
     peers = {o: (clu, lax.rem(me + o, SMP)) for o in range(1, SMP)}
+    has_after, has_before = device < CLU * SMP - 1, device > 0
+    has_up, has_down = clu < CLU - 1, clu > 0
 
     barrier = pltpu.get_barrier_semaphore()
-    for where in (after_id, before_id, up_id, down_id, *peers.values()):
+
+    def greet(where):
         pl.semaphore_signal(barrier, inc=1, device_id=where, device_id_type=MESH)
+
+    greeted = SMP - 1
+    for there, where in (
+        (has_after, after_id),
+        (has_before, before_id),
+        (has_up, up_id),
+        (has_down, down_id),
+    ):
+        pl.when(there)(functools.partial(greet, where))
+        greeted = greeted + there.astype(I32)
+    for where in peers.values():
+        greet(where)
 
     columns = pl.ds(pl.multiple_of(me * 128, 128), 128)
     loads = [
@@ -172,7 +188,17 @@
     near_cur[1, 0] = xall[me, :, 0, :].astype(BF16)
     near_cur[1, 1] = xall[me, :, 1, :].astype(BF16)
 
-    pl.semaphore_wait(barrier, 4 + SMP - 1)
+    def clear(near_slot, up_slot):
+        if near_slot is not None:
+            near_cur[near_slot] = jnp.zeros((2, LEAF, 128), BF16)
+        if up_slot is not None:
+            upper[up_slot] = jnp.zeros((2, PAR, 128), F32)
+
+    pl.when(jnp.logical_not(has_before))(functools.partial(clear, 0, None))
+    pl.when(jnp.logical_not(has_after))(functools.partial(clear, 2, None))
+    pl.when(jnp.logical_not(has_down))(functools.partial(clear, None, 0))
+    pl.when(jnp.logical_not(has_up))(functools.partial(clear, None, 2))
+    pl.semaphore_wait(barrier, greeted)
     near_out = [
         pltpu.make_async_remote_copy(
             src_ref=near_cur.at[1],
@@ -184,8 +210,8 @@
         )
         for i, (slot, where) in enumerate(((0, after_id), (2, before_id)))
     ]
-    for copy in near_out:
-        copy.start()
+    for copy, there in zip(near_out, (has_after, has_before)):
+        pl.when(there)(copy.start)
     cur_out = [
         pltpu.make_async_remote_copy(
             src_ref=xall.at[me],
@@ -203,7 +229,7 @@
     for copy in copies[1:9]:
         copy.wait()
     grid = itp_v[...]
-    both = mm(rad_v[...].reshape(256, 256), grid, NN, HIGHEST)
+    both = mm(split3(rad_v[...].reshape(256, 256)), stacked(grid))
     m_op[...] = stacked(complex_square(both[:128], both[128:]))
     both = mm(grid, jnp.concatenate([rec_v[0], rec_v[1]], axis=1), TN, HIGHEST)
     n_op[...] = stacked(complex_square(both[:, :128], both[:, 128:]))
@@ -224,8 +250,8 @@
     t_re[...] = tr_v[:, 0, :]
     t_im[...] = tr_v[:, 1, :]
 
-    for copy in near_out:
-        copy.wait_recv()
+    for copy, there in zip(near_out, (has_before, has_after)):
+        pl.when(there)(copy.wait_recv)
     p_re = near_cur[:, 0].reshape(PAR, 128).astype(F32)
     p_im = near_cur[:, 1].reshape(PAR, 128).astype(F32)
     sources = jnp.concatenate(
@@ -245,23 +271,25 @@
 
     lane_leaf = lax.rem(iota((128, 128), 1), LEAF)
 
-    def near_chunk(i):
-        blk_copies[i].wait()
-        total = near_acc[...] if i else jnp.zeros((128, 128), F32)
+    def near_chunk(i, carry):
+        first = pl.multiple_of(i * CHUNK, CHUNK)
+        pltpu.make_async_copy(
+            blocks.at[pl.ds(first, CHUNK)], near_blk.at[pl.ds(first, CHUNK)], blk_sem.at[i]
+        ).wait()
         lhs = jnp.concatenate(
             [
-                near_blk[pl.ds(i * CHUNK, CHUNK), s, c].reshape(CHUNK * 128, 128)
+                near_blk[pl.ds(first, CHUNK), s, c].reshape(CHUNK * 128, 128)
                 for s in range(SLOTS)
                 for c in range(2)
             ],
             axis=1,
         )
         result = mm(lhs, near_x[...])
+        total = near_acc[...]
         for r in range(CHUNK):
-            total = jnp.where(
-                lane_leaf == i * CHUNK + r, result[r * 128 : (r + 1) * 128], total
-            )
+            total = jnp.where(lane_leaf == first + r, result[r * 128 : (r + 1) * 128], total)
         near_acc[...] = total
+        return carry
 
     for copy in cur_out:
         copy.wait_recv()
@@ -286,57 +314,45 @@
         )
         for i, (slot, where) in enumerate(((0, up_id), (2, down_id)))
     ]
-    for copy in up_out:
-        copy.start()
-
-    def translate(group, sums):
-        def word_step(turn, sums):
-            word = 3 * group + turn
-
-            def octet_step(step, sums):
-                sums = list(sums)
-                start = pl.multiple_of(32 * turn + 8 * step, 8)
-                up_re = upper[group, 0, pl.ds(start, 8)]
-                up_im = upper[group, 1, pl.ds(start, 8)]
-                offset = jnp.full((8, 128), 8 * step, I32)
-                marks = [
-                    lax.shift_right_logical(words[word, 8 * b : 8 * b + 8], offset)
-                    for b in range(BLOCKS)
-                ]
-                for i in range(8):
-                    source_re = jnp.broadcast_to(up_re[i : i + 1], (8, 128))
-                    source_im = jnp.broadcast_to(up_im[i : i + 1], (8, 128))
-                    for b in range(BLOCKS):
-                        at = 96 * group + start + (89 + i - 8 * b)
-                        op_re = t_re[pl.ds(at, 8)]
-                        op_im = t_im[pl.ds(at, 8)]
-                        there = (marks[b] & (1 << i)) != 0
-                        here_re = jnp.where(there, source_re, 0.0)
-                        here_im = jnp.where(there, source_im, 0.0)
-                        sums[2 * b] = sums[2 * b] + (op_re * here_re - op_im * here_im)
-                        sums[2 * b + 1] = sums[2 * b + 1] + (op_re * here_im + op_im * here_re)
-                return tuple(sums)
-
-            return lax.fori_loop(0, 4, octet_step, sums)
-
-        return lax.fori_loop(0, 3, word_step, sums)
-
-    sums = tuple(jnp.zeros((8, 128), F32) for _ in range(2 * BLOCKS))
-    sums = translate(1, sums)
-    near_chunk(0)
-    up_out[0].wait_recv()
-    sums = translate(0, sums)
-    up_out[1].wait_recv()
-    sums = translate(2, sums)
-
-    incoming = jnp.concatenate(
-        [jnp.concatenate(sums[0::2], axis=0), jnp.concatenate(sums[1::2], axis=0)], axis=1
-    )
-    field = mm(to_leaf[...], jnp.concatenate(halves(incoming), axis=0))
-    cos, sin = shift[:, :128], shift[:, 128:]
-    real, imag = field[:, :128], field[:, 128:]
-    back = jnp.concatenate([real * cos + imag * sin, imag * cos - real * sin], axis=1)
-    part[...] = mm(split3(back), n_op[...]).reshape(SMP, LEAF, 256)
+    for copy, there in zip(up_out, (has_up, has_down)):
+        pl.when(there)(copy.start)
+
+    def translate(group):
+        def octet_step(step, sums):
+            sums = list(sums)
+            start = pl.multiple_of(8 * step, 8)
+            up_re = upper[group, 0, pl.ds(start, 8)]
+            up_im = upper[group, 1, pl.ds(start, 8)]
+            offset = jnp.full((8, 128), 8 * lax.rem(step, 4), I32)
+            word = 3 * group + step // 4
+            marks = [
+                lax.shift_right_logical(words[word, 8 * b : 8 * b + 8], offset)
+                for b in range(BLOCKS)
+            ]
+            for i in range(8):
+                source_re = jnp.broadcast_to(up_re[i : i + 1], (8, 128))
+                source_im = jnp.broadcast_to(up_im[i : i + 1], (8, 128))
+                for b in range(BLOCKS):
+                    at = PAR * group + start + (89 + i - 8 * b)
+                    op_re = t_re[pl.ds(at, 8)]
+                    op_im = t_im[pl.ds(at, 8)]
+                    there = (marks[b] & (1 << i)) != 0
+                    here_re = jnp.where(there, source_re, 0.0)
+                    here_im = jnp.where(there, source_im, 0.0)
+                    sums[2 * b] = sums[2 * b] + (op_re * here_re - op_im * here_im)
+                    sums[2 * b + 1] = sums[2 * b + 1] + (op_re * here_im + op_im * here_re)
+            return tuple(sums)
+
+        sums = tuple(
+            incoming[8 * b : 8 * b + 8, 128 * c : 128 * c + 128]
+            for b in range(BLOCKS)
+            for c in range(2)
+        )
+        sums = lax.fori_loop(0, BLOCKS, octet_step, sums)
+        for b in range(BLOCKS):
+            for c in range(2):
+                incoming[8 * b : 8 * b + 8, 128 * c : 128 * c + 128] = sums[2 * b + c]
+
     part_out = [
         pltpu.make_async_remote_copy(
             src_ref=part.at[lax.rem(me + o, SMP)],
@@ -348,10 +364,33 @@
         )
         for o in ORDER
     ]
-    for copy in part_out:
-        copy.start()
-    for i in range(1, CHUNKS):
-        near_chunk(i)
+
+    def spread():
+        field = mm(to_leaf[...], jnp.concatenate(halves(incoming[...]), axis=0))
+        cos, sin = shift[:, :128], shift[:, 128:]
+        real, imag = field[:, :128], field[:, 128:]
+        back = jnp.concatenate([real * cos + imag * sin, imag * cos - real * sin], axis=1)
+        part[...] = mm(split3(back), n_op[...]).reshape(SMP, LEAF, 256)
+        for copy in part_out:
+            copy.start()
+
+    incoming[...] = jnp.zeros((PAR, 256), F32)
+    near_acc[...] = jnp.zeros((128, 128), F32)
+
+    order = jnp.where(lax.rem(clu, 4) == 0, 1, 2)
+
+    def phase(turn, carry):
+        group = lax.rem(1 + order * turn, 3)
+        pl.when((group == 0) & has_down)(up_out[0].wait_recv)
+        pl.when((group == 2) & has_up)(up_out[1].wait_recv)
+        translate(group)
+        pl.when(turn == 2)(spread)
+        lax.fori_loop(
+            jnp.minimum(turn, 1), jnp.where(turn == 2, CHUNKS, 1), near_chunk, 0
+        )
+        return carry
+
+    lax.fori_loop(0, 3, phase, 0)
     near = near_acc[...].T
     total = part[me] + jnp.concatenate([near[:LEAF], near[LEAF : 2 * LEAF]], axis=1)
     for copy, o in zip(part_out, ORDER):
@@ -359,7 +398,9 @@
         total = total + arrived[o - 1]
     out[:, 0, :] = total[:, :128]
     out[:, 1, :] = total[:, 128:]
-    for copy in (*near_out, *cur_out, *up_out, *part_out):
+    for copy, there in zip((*near_out, *up_out), (has_after, has_before, has_up, has_down)):
+        pl.when(there)(copy.wait_send)
+    for copy in (*cur_out, *part_out):
         copy.wait_send()
 
 
@@ -382,7 +423,7 @@
     dma = pltpu.SemaphoreType.DMA
     return pl.pallas_call(
         body,
-        out_shape=jax.ShapeDtypeStruct((LEAF, 2, 128), F32),
+        out_shape=vmem((LEAF, 2, 128), F32),
         in_specs=[hbm_spec] * 11,
         out_specs=pl.BlockSpec(memory_space=vmem),
         scratch_shapes=[
@@ -409,6 +450,7 @@
             vmem((WORDS, PAR, 128), I32),
             vmem((SLOTS * 256, 128), BF16),
             vmem((128, 128), F32),
+            vmem((PAR, 256), F32),
             vmem((SMP, LEAF, 256), F32),
             vmem((SMP - 1, LEAF, 256), F32),
             dma((11,)),
@@ -423,7 +465,7 @@
             dma((SMP - 1,)),
         ],
         compiler_params=pltpu.CompilerParams(
-            collective_id=0, has_side_effects=True, vmem_limit_bytes=48 * 1024 * 1024
+            collective_id=0, has_side_effects=True, vmem_limit_bytes=60 * 1024 * 1024
         ),
         name="far_and_near",
     )(

time: 38.8 us -> 25.3 us (0.65)
  the two profiles are of different devices: /device:TPU:1 before, /device:TPU:25 now
where the time goes in v2:
time: 25.3 us; the launch traced here: 24.8 us
  Pallas kernels  24.2 us (96%)
  local copies, waits for them, and re-layouts  0.62 us (2%)
    pallas_call x1, Pallas kernels, on_device(): pl.pallas_call(body, out_shape=vmem((LEAF, 2, 128), F32), in_specs=[hbm_s...  24.2 us
    unnamed x1, local copies, waits for them, and re-layouts  0.62 us

profile of v2, /device:TPU:25, one launch (start us, length us, event | category | flops | bytes accessed | tf_op | source)
XLA Modules:
  0.0 24.8 jit_solution(14568353113367196444)
XLA Ops:
  0.0 24.2 %far_and_near.1 = f32[32,2,128]{2,1,0:T(2,128)S(1)} custom-call(f32[32,2,128]{2,1,0:T(2,128)} %cur.1, bf16[32,6,2,128,128]{4,3,2,1,0:T(8,128)(2,1)} %blocks.1, s32[6,32]{1,0:T(8,128)} %bitcast.3, f32[2,128,256]{2,1,0:T(8,128)} %rad.1, f32[256,1024]{1,0:T(8,128)} %itp.1, f32[8,1024]{1,0:T(8,128)} %phase.1, s32[1,256]{1,0:T(1,128)} %pmap.1, s32[1,256]{1,0:T(1,128)} %octant.1, ...), custom_call_target="tpu_custom_call" | custom-call | tf_op jit(solution)/shard_map/far_and_near/pallas_call | solution.py:424
  24.2 0.6 %copy.13 = f32[32,2,128]{2,1,0:T(2,128)} copy(f32[32,2,128]{2,1,0:T(2,128)S(1)} %far_and_near.1) | data formatting | bytes 65536

commit v3 on v2

--- a/solution.py
+++ b/solution.py
@@ -28,6 +28,7 @@
 WORDS = 9
 CHUNK = 8
 CHUNKS = LEAF // CHUNK
+STEPS = 32000.0
 ORDER = (4, 3, 5, 2, 6, 1, 7)
 
 
@@ -52,6 +53,27 @@
 def split3(value):
     high, low = halves(value)
     return jnp.concatenate([high, high, low], axis=1)
+
+
+def coded(value):
+    top = jnp.maximum(jnp.max(jnp.abs(value), axis=0, keepdims=True), 1e-30)
+    power = jnp.ceil(jnp.log2(top))
+    whole = jnp.floor(value * (STEPS * jnp.exp2(-power)) + 0.5)
+    return whole.astype(I32), power
+
+
+def message(parts):
+    pairs = [coded(part) for part in parts]
+    tail = [jnp.broadcast_to(power, (8, 128)).astype(I32) for _, power in pairs]
+    return jnp.concatenate([whole for whole, _ in pairs] + tail, axis=0).astype(jnp.int16)
+
+
+def decoded(block, rows):
+    value = block.astype(I32).astype(F32)
+    scale = [
+        jnp.exp2(value[2 * rows + 8 * c : 2 * rows + 8 * c + 1]) * (1.0 / STEPS) for c in range(2)
+    ]
+    return [value[c * rows : (c + 1) * rows] * scale[c] for c in range(2)]
 
 
 def complex_square(real, imag):
@@ -88,7 +110,8 @@
     far_src,
     rec,
     out,
-    xall,
+    cur_v,
+    cur_msg,
     near_cur,
     near_blk,
     ns_v,
@@ -103,6 +126,7 @@
     t_re,
     t_im,
     upper,
+    up_msg,
     m_op,
     n_op,
     shift,
@@ -113,6 +137,7 @@
     near_acc,
     incoming,
     part,
+    part_msg,
     arrived,
     load_sem,
     blk_sem,
@@ -157,7 +182,7 @@
 
     columns = pl.ds(pl.multiple_of(me * 128, 128), 128)
     loads = [
-        (cur, xall.at[me]),
+        (cur, cur_v),
         (itp.at[:, columns], itp_v),
         (phase.at[:, columns], ph_v),
         (rad, rad_v),
@@ -185,14 +210,16 @@
         copy.start()
 
     copies[0].wait()
-    near_cur[1, 0] = xall[me, :, 0, :].astype(BF16)
-    near_cur[1, 1] = xall[me, :, 1, :].astype(BF16)
+    own_cur = [cur_v[:, c, :] for c in range(2)]
+    for c in range(2):
+        near_cur[1, c] = own_cur[c].astype(BF16)
+    cur_msg[me] = message(own_cur)
 
     def clear(near_slot, up_slot):
         if near_slot is not None:
             near_cur[near_slot] = jnp.zeros((2, LEAF, 128), BF16)
         if up_slot is not None:
-            upper[up_slot] = jnp.zeros((2, PAR, 128), F32)
+            up_msg[up_slot] = jnp.zeros((2 * PAR + 16, 128), jnp.int16)
 
     pl.when(jnp.logical_not(has_before))(functools.partial(clear, 0, None))
     pl.when(jnp.logical_not(has_after))(functools.partial(clear, 2, None))
@@ -210,12 +237,10 @@
         )
         for i, (slot, where) in enumerate(((0, after_id), (2, before_id)))
     ]
-    for copy, there in zip(near_out, (has_after, has_before)):
-        pl.when(there)(copy.start)
     cur_out = [
         pltpu.make_async_remote_copy(
-            src_ref=xall.at[me],
-            dst_ref=xall.at[me],
+            src_ref=cur_msg.at[me],
+            dst_ref=cur_msg.at[me],
             send_sem=cur_send.at[o - 1],
             recv_sem=cur_recv.at[o - 1],
             device_id=peers[o],
@@ -225,6 +250,8 @@
     ]
     for copy in cur_out:
         copy.start()
+    for copy, there in zip(near_out, (has_after, has_before)):
+        pl.when(there)(copy.start)
 
     for copy in copies[1:9]:
         copy.wait()
@@ -250,25 +277,6 @@
     t_re[...] = tr_v[:, 0, :]
     t_im[...] = tr_v[:, 1, :]
 
-    for copy, there in zip(near_out, (has_before, has_after)):
-        pl.when(there)(copy.wait_recv)
-    p_re = near_cur[:, 0].reshape(PAR, 128).astype(F32)
-    p_im = near_cur[:, 1].reshape(PAR, 128).astype(F32)
-    sources = jnp.concatenate(
-        [jnp.concatenate([p_re, -p_im], axis=1), jnp.concatenate([p_im, p_re], axis=1)], axis=0
-    )
-    local = ns_v[...] - (device - 1) * LEAF
-    local = jnp.concatenate(
-        [local, local + PAR, jnp.full((SLOTS, 64), -1, I32)], axis=1
-    )
-    rows = iota((2 * PAR, 128), 0)
-    picks = jnp.concatenate(
-        [(local[s : s + 1] == rows).astype(F32) for s in range(SLOTS)], axis=1
-    ).astype(BF16)
-    rhs = mm(sources.T.astype(BF16), picks).astype(BF16)
-    for s in range(SLOTS):
-        near_x[pl.ds(s * 256, 256)] = rhs[:, s * 128 : (s + 1) * 128]
-
     lane_leaf = lax.rem(iota((128, 128), 1), LEAF)
 
     def near_chunk(i, carry):
@@ -294,19 +302,21 @@
     for copy in cur_out:
         copy.wait_recv()
     x = jnp.concatenate(
-        [xall[:, :, 0, :].reshape(GROUP, 128), xall[:, :, 1, :].reshape(GROUP, 128)], axis=1
+        [jnp.concatenate(decoded(cur_msg[i], LEAF), axis=1) for i in range(SMP)], axis=0
     )
     inter = mm(split3(x), m_op[...])
     cos, sin = shift[:, :128], shift[:, 128:]
     real, imag = inter[:, :128], inter[:, 128:]
     shifted = jnp.concatenate([real * cos - imag * sin, real * sin + imag * cos], axis=1)
     own = mm(to_parent[...], jnp.concatenate(halves(shifted), axis=0))
-    upper[1, 0] = own[:, :128]
-    upper[1, 1] = own[:, 128:]
+    own = [own[:, :128], own[:, 128:]]
+    for c in range(2):
+        upper[1, c] = own[c]
+    up_msg[1] = message(own)
     up_out = [
         pltpu.make_async_remote_copy(
-            src_ref=upper.at[1],
-            dst_ref=upper.at[slot],
+            src_ref=up_msg.at[1],
+            dst_ref=up_msg.at[slot],
             send_sem=up_send.at[i],
             recv_sem=up_recv.at[i],
             device_id=where,
@@ -316,6 +326,25 @@
     ]
     for copy, there in zip(up_out, (has_up, has_down)):
         pl.when(there)(copy.start)
+
+    for copy, there in zip(near_out, (has_before, has_after)):
+        pl.when(there)(copy.wait_recv)
+    p_re = near_cur[:, 0].reshape(PAR, 128).astype(F32)
+    p_im = near_cur[:, 1].reshape(PAR, 128).astype(F32)
+    sources = jnp.concatenate(
+        [jnp.concatenate([p_re, -p_im], axis=1), jnp.concatenate([p_im, p_re], axis=1)], axis=0
+    )
+    local = ns_v[...] - (device - 1) * LEAF
+    local = jnp.concatenate(
+        [local, local + PAR, jnp.full((SLOTS, 64), -1, I32)], axis=1
+    )
+    rows = iota((2 * PAR, 128), 0)
+    picks = jnp.concatenate(
+        [(local[s : s + 1] == rows).astype(F32) for s in range(SLOTS)], axis=1
+    ).astype(BF16)
+    rhs = mm(sources.T.astype(BF16), picks).astype(BF16)
+    for s in range(SLOTS):
+        near_x[pl.ds(s * 256, 256)] = rhs[:, s * 128 : (s + 1) * 128]
 
     def translate(group):
         def octet_step(step, sums):
@@ -355,7 +384,7 @@
 
     part_out = [
         pltpu.make_async_remote_copy(
-            src_ref=part.at[lax.rem(me + o, SMP)],
+            src_ref=part_msg.at[lax.rem(me + o, SMP)],
             dst_ref=arrived.at[o - 1],
             send_sem=part_send.at[o - 1],
             recv_sem=part_recv.at[o - 1],
@@ -370,7 +399,11 @@
         cos, sin = shift[:, :128], shift[:, 128:]
         real, imag = field[:, :128], field[:, 128:]
         back = jnp.concatenate([real * cos + imag * sin, imag * cos - real * sin], axis=1)
-        part[...] = mm(split3(back), n_op[...]).reshape(SMP, LEAF, 256)
+        result = mm(split3(back), n_op[...])
+        part[...] = result.reshape(SMP, LEAF, 256)
+        for i in range(SMP):
+            rows = result[i * LEAF : (i + 1) * LEAF]
+            part_msg[i] = message([rows[:, :128], rows[:, 128:]])
         for copy in part_out:
             copy.start()
 
@@ -383,6 +416,12 @@
         group = lax.rem(1 + order * turn, 3)
         pl.when((group == 0) & has_down)(up_out[0].wait_recv)
         pl.when((group == 2) & has_up)(up_out[1].wait_recv)
+
+        @pl.when(turn > 0)
+        def take():
+            for c, value in enumerate(decoded(up_msg[group], PAR)):
+                upper[group, c] = value
+
         translate(group)
         pl.when(turn == 2)(spread)
         lax.fori_loop(
@@ -395,7 +434,7 @@
     total = part[me] + jnp.concatenate([near[:LEAF], near[LEAF : 2 * LEAF]], axis=1)
     for copy, o in zip(part_out, ORDER):
         copy.wait_recv()
-        total = total + arrived[o - 1]
+        total = total + jnp.concatenate(decoded(arrived[o - 1], LEAF), axis=1)
     out[:, 0, :] = total[:, :128]
     out[:, 1, :] = total[:, 128:]
     for copy, there in zip((*near_out, *up_out), (has_after, has_before, has_up, has_down)):
@@ -427,7 +466,8 @@
         in_specs=[hbm_spec] * 11,
         out_specs=pl.BlockSpec(memory_space=vmem),
         scratch_shapes=[
-            vmem((SMP, LEAF, 2, 128), F32),
+            vmem((LEAF, 2, 128), F32),
+            vmem((SMP, 2 * LEAF + 16, 128), jnp.int16),
             vmem((3, 2, LEAF, 128), BF16),
             vmem((LEAF, SLOTS, 2, 128, 128), BF16),
             vmem((SLOTS, LEAF), I32),
@@ -442,6 +482,7 @@
             vmem((TABLE, 128), F32),
             vmem((TABLE, 128), F32),
             vmem((3, 2, PAR, 128), F32),
+            vmem((3, 2 * PAR + 16, 128), jnp.int16),
             vmem((768, 256), BF16),
             vmem((768, 256), BF16),
             vmem((GROUP, 256), F32),
@@ -452,7 +493,8 @@
             vmem((128, 128), F32),
             vmem((PAR, 256), F32),
             vmem((SMP, LEAF, 256), F32),
-            vmem((SMP - 1, LEAF, 256), F32),
+            vmem((SMP, 2 * LEAF + 16, 128), jnp.int16),
+            vmem((SMP - 1, 2 * LEAF + 16, 128), jnp.int16),
             dma((11,)),
             dma((CHUNKS,)),
             dma((2,)),

time: 25.3 us -> 23.7 us (0.937); the launches traced: 24.8 us -> 23.6 us
  Pallas kernels: 24.2 us -> 23 us
    pallas_call x1, Pallas kernels: 24.2 us -> 23 us  [on_device(): pl.pallas_call(body, out_shape=vmem((LEAF, 2, 128), F32), in_specs=[hbm_s...]
where the time goes in v3:
time: 23.7 us; the launch traced here: 23.6 us
  Pallas kernels  23 us (97%)
  local copies, waits for them, and re-layouts  0.62 us (3%)
    pallas_call x1, Pallas kernels, on_device(): pl.pallas_call(body, out_shape=vmem((LEAF, 2, 128), F32), in_specs=[hbm_s...  23 us
    unnamed x1, local copies, waits for them, and re-layouts  0.62 us

profile of v3, /device:TPU:25, one launch (start us, length us, event | category | flops | bytes accessed | tf_op | source)
XLA Modules:
  0.0 23.6 jit_solution(17091685454257801213)
XLA Ops:
  0.0 23.0 %far_and_near.1 = f32[32,2,128]{2,1,0:T(2,128)S(1)} custom-call(f32[32,2,128]{2,1,0:T(2,128)} %cur.1, bf16[32,6,2,128,128]{4,3,2,1,0:T(8,128)(2,1)} %blocks.1, s32[6,32]{1,0:T(8,128)} %bitcast.3, f32[2,128,256]{2,1,0:T(8,128)} %rad.1, f32[256,1024]{1,0:T(8,128)} %itp.1, f32[8,1024]{1,0:T(8,128)} %phase.1, s32[1,256]{1,0:T(1,128)} %pmap.1, s32[1,256]{1,0:T(1,128)} %octant.1, ...), custom_call_target="tpu_custom_call" | custom-call | tf_op jit(solution)/shard_map/far_and_near/pallas_call | solution.py:463
  23.0 0.6 %copy.13 = f32[32,2,128]{2,1,0:T(2,128)} copy(f32[32,2,128]{2,1,0:T(2,128)S(1)} %far_and_near.1) | data formatting | bytes 65536

commit v4 on v3

--- a/solution.py
+++ b/solution.py
@@ -149,6 +149,8 @@
     up_recv,
     part_send,
     part_recv,
+    up_greet,
+    near_greet,
 ):
     clu = lax.axis_index("clu")
     me = lax.axis_index("smp")
@@ -168,15 +170,20 @@
     def greet(where):
         pl.semaphore_signal(barrier, inc=1, device_id=where, device_id_type=MESH)
 
+    defers = (lax.rem(clu, 4) == 0) & has_down
+    late = (lax.rem(clu, 4) == 3) & has_up
+    near_defers = defers & (me == 0)
+    near_late = late & (me == SMP - 1)
+
     greeted = SMP - 1
-    for there, where in (
-        (has_after, after_id),
-        (has_before, before_id),
-        (has_up, up_id),
-        (has_down, down_id),
+    for to, from_, where in (
+        (has_after & jnp.logical_not(near_late), has_after, after_id),
+        (has_before, has_before & jnp.logical_not(near_defers), before_id),
+        (has_up & jnp.logical_not(late), has_up, up_id),
+        (has_down, has_down & jnp.logical_not(defers), down_id),
     ):
-        pl.when(there)(functools.partial(greet, where))
-        greeted = greeted + there.astype(I32)
+        pl.when(to)(functools.partial(greet, where))
+        greeted = greeted + from_.astype(I32)
     for where in peers.values():
         greet(where)
 
@@ -226,6 +233,14 @@
     pl.when(jnp.logical_not(has_down))(functools.partial(clear, None, 0))
     pl.when(jnp.logical_not(has_up))(functools.partial(clear, None, 2))
     pl.semaphore_wait(barrier, greeted)
+
+    def called(there, semaphore, where):
+        @pl.when(there)
+        def call():
+            pl.semaphore_signal(semaphore, inc=1, device_id=where, device_id_type=MESH)
+
+    called(late, up_greet, up_id)
+    called(near_late, near_greet, after_id)
     near_out = [
         pltpu.make_async_remote_copy(
             src_ref=near_cur.at[1],
@@ -250,7 +265,7 @@
     ]
     for copy in cur_out:
         copy.start()
-    for copy, there in zip(near_out, (has_after, has_before)):
+    for copy, there in zip(near_out, (has_after, has_before & jnp.logical_not(near_defers))):
         pl.when(there)(copy.start)
 
     for copy in copies[1:9]:
@@ -324,27 +339,18 @@
         )
         for i, (slot, where) in enumerate(((0, up_id), (2, down_id)))
     ]
-    for copy, there in zip(up_out, (has_up, has_down)):
-        pl.when(there)(copy.start)
-
-    for copy, there in zip(near_out, (has_before, has_after)):
-        pl.when(there)(copy.wait_recv)
-    p_re = near_cur[:, 0].reshape(PAR, 128).astype(F32)
-    p_im = near_cur[:, 1].reshape(PAR, 128).astype(F32)
-    sources = jnp.concatenate(
-        [jnp.concatenate([p_re, -p_im], axis=1), jnp.concatenate([p_im, p_re], axis=1)], axis=0
-    )
-    local = ns_v[...] - (device - 1) * LEAF
-    local = jnp.concatenate(
-        [local, local + PAR, jnp.full((SLOTS, 64), -1, I32)], axis=1
-    )
-    rows = iota((2 * PAR, 128), 0)
-    picks = jnp.concatenate(
-        [(local[s : s + 1] == rows).astype(F32) for s in range(SLOTS)], axis=1
-    ).astype(BF16)
-    rhs = mm(sources.T.astype(BF16), picks).astype(BF16)
-    for s in range(SLOTS):
-        near_x[pl.ds(s * 256, 256)] = rhs[:, s * 128 : (s + 1) * 128]
+    pl.when(has_up)(up_out[0].start)
+
+    @pl.when(defers)
+    def await_late():
+        pl.semaphore_wait(up_greet, 1)
+
+    pl.when(has_down)(up_out[1].start)
+
+    @pl.when(near_defers)
+    def await_near_late():
+        pl.semaphore_wait(near_greet, 1)
+        near_out[1].start()
 
     def translate(group):
         def octet_step(step, sums):
@@ -424,12 +430,30 @@
 
         translate(group)
         pl.when(turn == 2)(spread)
-        lax.fori_loop(
-            jnp.minimum(turn, 1), jnp.where(turn == 2, CHUNKS, 1), near_chunk, 0
-        )
         return carry
 
     lax.fori_loop(0, 3, phase, 0)
+
+    for copy, there in zip(near_out, (has_before, has_after)):
+        pl.when(there)(copy.wait_recv)
+    p_re = near_cur[:, 0].reshape(PAR, 128).astype(F32)
+    p_im = near_cur[:, 1].reshape(PAR, 128).astype(F32)
+    sources = jnp.concatenate(
+        [jnp.concatenate([p_re, -p_im], axis=1), jnp.concatenate([p_im, p_re], axis=1)], axis=0
+    )
+    local = ns_v[...] - (device - 1) * LEAF
+    local = jnp.concatenate(
+        [local, local + PAR, jnp.full((SLOTS, 64), -1, I32)], axis=1
+    )
+    rows = iota((2 * PAR, 128), 0)
+    picks = jnp.concatenate(
+        [(local[s : s + 1] == rows).astype(F32) for s in range(SLOTS)], axis=1
+    ).astype(BF16)
+    rhs = mm(sources.T.astype(BF16), picks).astype(BF16)
+    for s in range(SLOTS):
+        near_x[pl.ds(s * 256, 256)] = rhs[:, s * 128 : (s + 1) * 128]
+
+    lax.fori_loop(0, CHUNKS, near_chunk, 0)
     near = near_acc[...].T
     total = part[me] + jnp.concatenate([near[:LEAF], near[LEAF : 2 * LEAF]], axis=1)
     for copy, o in zip(part_out, ORDER):
@@ -505,6 +529,8 @@
             dma((2,)),
             dma((SMP - 1,)),
             dma((SMP - 1,)),
+            pltpu.SemaphoreType.REGULAR,
+            pltpu.SemaphoreType.REGULAR,
         ],
         compiler_params=pltpu.CompilerParams(
             collective_id=0, has_side_effects=True, vmem_limit_bytes=60 * 1024 * 1024

time: 23.7 us -> 22.7 us (0.958)
  the two profiles are of different devices: /device:TPU:25 before, /device:TPU:1 now
where the time goes in v4:
time: 22.7 us; the launch traced here: 22.6 us
  Pallas kernels  21.9 us (96%)
  local copies, waits for them, and re-layouts  0.62 us (3%)
    pallas_call x1, Pallas kernels, on_device(): pl.pallas_call(body, out_shape=vmem((LEAF, 2, 128), F32), in_specs=[hbm_s...  21.9 us
    unnamed x1, local copies, waits for them, and re-layouts  0.62 us

profile of v4, /device:TPU:1, one launch (start us, length us, event | category | flops | bytes accessed | tf_op | source)
XLA Modules:
  0.0 22.6 jit_solution(13397475065648484496)
XLA Ops:
  0.0 21.9 %far_and_near.1 = f32[32,2,128]{2,1,0:T(2,128)S(1)} custom-call(f32[32,2,128]{2,1,0:T(2,128)} %cur.1, bf16[32,6,2,128,128]{4,3,2,1,0:T(8,128)(2,1)} %blocks.1, s32[6,32]{1,0:T(8,128)} %bitcast.3, f32[2,128,256]{2,1,0:T(8,128)} %rad.1, f32[256,1024]{1,0:T(8,128)} %itp.1, f32[8,1024]{1,0:T(8,128)} %phase.1, s32[1,256]{1,0:T(1,128)} %pmap.1, s32[1,256]{1,0:T(1,128)} %octant.1, ...), custom_call_target="tpu_custom_call" | custom-call | tf_op jit(solution)/shard_map/far_and_near/pallas_call | solution.py:487
  22.0 0.6 %copy.13 = f32[32,2,128]{2,1,0:T(2,128)} copy(f32[32,2,128]{2,1,0:T(2,128)S(1)} %far_and_near.1) | data formatting | bytes 65536

commit v5 on v4

--- a/solution.py
+++ b/solution.py
@@ -28,6 +28,7 @@
 WORDS = 9
 CHUNK = 8
 CHUNKS = LEAF // CHUNK
+EARLY = 1
 STEPS = 32000.0
 ORDER = (4, 3, 5, 2, 6, 1, 7)
 
@@ -383,7 +384,10 @@
             for b in range(BLOCKS)
             for c in range(2)
         )
-        sums = lax.fori_loop(0, BLOCKS, octet_step, sums)
+        def octet_pair(pair, sums):
+            return octet_step(2 * pair + 1, octet_step(2 * pair, sums))
+
+        sums = lax.fori_loop(0, BLOCKS // 2, octet_pair, sums)
         for b in range(BLOCKS):
             for c in range(2):
                 incoming[8 * b : 8 * b + 8, 128 * c : 128 * c + 128] = sums[2 * b + c]
@@ -416,44 +420,57 @@
     incoming[...] = jnp.zeros((PAR, 256), F32)
     near_acc[...] = jnp.zeros((128, 128), F32)
 
+    def near_sides():
+        for copy, there in zip(near_out, (has_before, has_after)):
+            pl.when(there)(copy.wait_recv)
+        p_re = near_cur[:, 0].reshape(PAR, 128).astype(F32)
+        p_im = near_cur[:, 1].reshape(PAR, 128).astype(F32)
+        sources = jnp.concatenate(
+            [jnp.concatenate([p_re, -p_im], axis=1), jnp.concatenate([p_im, p_re], axis=1)], axis=0
+        )
+        local = ns_v[...] - (device - 1) * LEAF
+        local = jnp.concatenate(
+            [local, local + PAR, jnp.full((SLOTS, 64), -1, I32)], axis=1
+        )
+        rows = iota((2 * PAR, 128), 0)
+        picks = jnp.concatenate(
+            [(local[s : s + 1] == rows).astype(F32) for s in range(SLOTS)], axis=1
+        ).astype(BF16)
+        rhs = mm(sources.T.astype(BF16), picks).astype(BF16)
+        for s in range(SLOTS):
+            near_x[pl.ds(s * 256, 256)] = rhs[:, s * 128 : (s + 1) * 128]
+
     order = jnp.where(lax.rem(clu, 4) == 0, 1, 2)
+
+    ahead = jnp.where(lax.rem(clu, 4) == 0, EARLY, 0)
+    sides_at = jnp.where(lax.rem(clu, 4) == 0, 0, 2)
 
     def phase(turn, carry):
         group = lax.rem(1 + order * turn, 3)
         pl.when((group == 0) & has_down)(up_out[0].wait_recv)
         pl.when((group == 2) & has_up)(up_out[1].wait_recv)
+        missing = ((group == 0) & jnp.logical_not(has_down)) | (
+            (group == 2) & jnp.logical_not(has_up)
+        )
 
         @pl.when(turn > 0)
         def take():
             for c, value in enumerate(decoded(up_msg[group], PAR)):
                 upper[group, c] = value
 
-        translate(group)
+        pl.when(jnp.logical_not(missing))(functools.partial(translate, group))
         pl.when(turn == 2)(spread)
+        pl.when(turn == sides_at)(near_sides)
+        lax.fori_loop(
+            jnp.where(turn == 0, 0, ahead),
+            jnp.where(turn == 2, CHUNKS, ahead),
+            near_chunk,
+            0,
+        )
         return carry
 
     lax.fori_loop(0, 3, phase, 0)
 
-    for copy, there in zip(near_out, (has_before, has_after)):
-        pl.when(there)(copy.wait_recv)
-    p_re = near_cur[:, 0].reshape(PAR, 128).astype(F32)
-    p_im = near_cur[:, 1].reshape(PAR, 128).astype(F32)
-    sources = jnp.concatenate(
-        [jnp.concatenate([p_re, -p_im], axis=1), jnp.concatenate([p_im, p_re], axis=1)], axis=0
-    )
-    local = ns_v[...] - (device - 1) * LEAF
-    local = jnp.concatenate(
-        [local, local + PAR, jnp.full((SLOTS, 64), -1, I32)], axis=1
-    )
-    rows = iota((2 * PAR, 128), 0)
-    picks = jnp.concatenate(
-        [(local[s : s + 1] == rows).astype(F32) for s in range(SLOTS)], axis=1
-    ).astype(BF16)
-    rhs = mm(sources.T.astype(BF16), picks).astype(BF16)
-    for s in range(SLOTS):
-        near_x[pl.ds(s * 256, 256)] = rhs[:, s * 128 : (s + 1) * 128]
-
-    lax.fori_loop(0, CHUNKS, near_chunk, 0)
     near = near_acc[...].T
     total = part[me] + jnp.concatenate([near[:LEAF], near[LEAF : 2 * LEAF]], axis=1)
     for copy, o in zip(part_out, ORDER):

time: 22.7 us -> 22 us (0.969)
  the two profiles are of different devices: /device:TPU:1 before, /device:TPU:25 now
where the time goes in v5:
time: 22 us; the launch traced here: 21.9 us
  Pallas kernels  21.3 us (97%)
  local copies, waits for them, and re-layouts  0.62 us (3%)
    pallas_call x1, Pallas kernels, on_device(): pl.pallas_call(body, out_shape=vmem((LEAF, 2, 128), F32), in_specs=[hbm_s...  21.3 us
    unnamed x1, local copies, waits for them, and re-layouts  0.62 us

profile of v5, /device:TPU:25, one launch (start us, length us, event | category | flops | bytes accessed | tf_op | source)
XLA Modules:
  0.0 21.9 jit_solution(428734844456740451)
XLA Ops:
  0.0 21.3 %far_and_near.1 = f32[32,2,128]{2,1,0:T(2,128)S(1)} custom-call(f32[32,2,128]{2,1,0:T(2,128)} %cur.1, bf16[32,6,2,128,128]{4,3,2,1,0:T(8,128)(2,1)} %blocks.1, s32[6,32]{1,0:T(8,128)} %bitcast.3, f32[2,128,256]{2,1,0:T(8,128)} %rad.1, f32[256,1024]{1,0:T(8,128)} %itp.1, f32[8,1024]{1,0:T(8,128)} %phase.1, s32[1,256]{1,0:T(1,128)} %pmap.1, s32[1,256]{1,0:T(1,128)} %octant.1, ...), custom_call_target="tpu_custom_call" | custom-call | tf_op jit(solution)/shard_map/far_and_near/pallas_call | solution.py:504
  21.3 0.6 %copy.13 = f32[32,2,128]{2,1,0:T(2,128)} copy(f32[32,2,128]{2,1,0:T(2,128)S(1)} %far_and_near.1) | data formatting | bytes 65536

commit v6 on v5

--- a/solution.py
+++ b/solution.py
@@ -125,7 +125,8 @@
     fs_v,
     rec_v,
     t_re,
-    t_im,
+    t_minus,
+    t_plus,
     upper,
     up_msg,
     m_op,
@@ -266,7 +267,8 @@
     ]
     for copy in cur_out:
         copy.start()
-    for copy, there in zip(near_out, (has_after, has_before & jnp.logical_not(near_defers))):
+    across = (has_after & (me == SMP - 1), has_before & (me == 0) & jnp.logical_not(near_defers))
+    for copy, there in zip(near_out, across):
         pl.when(there)(copy.start)
 
     for copy in copies[1:9]:
@@ -291,7 +293,8 @@
     copies[9].wait()
     copies[10].wait()
     t_re[...] = tr_v[:, 0, :]
-    t_im[...] = tr_v[:, 1, :]
+    t_minus[...] = tr_v[:, 1, :] - tr_v[:, 0, :]
+    t_plus[...] = tr_v[:, 1, :] + tr_v[:, 0, :]
 
     lane_leaf = lax.rem(iota((128, 128), 1), LEAF)
 
@@ -348,6 +351,9 @@
 
     pl.when(has_down)(up_out[1].start)
 
+    for copy, there in zip(near_out, (me < SMP - 1, me > 0)):
+        pl.when(there)(copy.start)
+
     @pl.when(near_defers)
     def await_near_late():
         pl.semaphore_wait(near_greet, 1)
@@ -368,29 +374,31 @@
             for i in range(8):
                 source_re = jnp.broadcast_to(up_re[i : i + 1], (8, 128))
                 source_im = jnp.broadcast_to(up_im[i : i + 1], (8, 128))
+                source_sum = source_re + source_im
                 for b in range(BLOCKS):
                     at = PAR * group + start + (89 + i - 8 * b)
                     op_re = t_re[pl.ds(at, 8)]
-                    op_im = t_im[pl.ds(at, 8)]
+                    op_minus = t_minus[pl.ds(at, 8)]
+                    op_plus = t_plus[pl.ds(at, 8)]
                     there = (marks[b] & (1 << i)) != 0
                     here_re = jnp.where(there, source_re, 0.0)
                     here_im = jnp.where(there, source_im, 0.0)
-                    sums[2 * b] = sums[2 * b] + (op_re * here_re - op_im * here_im)
-                    sums[2 * b + 1] = sums[2 * b + 1] + (op_re * here_im + op_im * here_re)
+                    here_sum = jnp.where(there, source_sum, 0.0)
+                    sums[3 * b] = sums[3 * b] + op_re * here_sum
+                    sums[3 * b + 1] = sums[3 * b + 1] + op_minus * here_re
+                    sums[3 * b + 2] = sums[3 * b + 2] + op_plus * here_im
             return tuple(sums)
 
-        sums = tuple(
-            incoming[8 * b : 8 * b + 8, 128 * c : 128 * c + 128]
-            for b in range(BLOCKS)
-            for c in range(2)
-        )
+        sums = tuple(jnp.zeros((8, 128), F32) for _ in range(3 * BLOCKS))
         def octet_pair(pair, sums):
             return octet_step(2 * pair + 1, octet_step(2 * pair, sums))
 
         sums = lax.fori_loop(0, BLOCKS // 2, octet_pair, sums)
         for b in range(BLOCKS):
-            for c in range(2):
-                incoming[8 * b : 8 * b + 8, 128 * c : 128 * c + 128] = sums[2 * b + c]
+            both, minus, plus = sums[3 * b : 3 * b + 3]
+            for c, value in enumerate((both - plus, both + minus)):
+                place = (pl.ds(8 * b, 8), pl.ds(128 * c, 128))
+                incoming[place] = incoming[place] + value
 
     part_out = [
         pltpu.make_async_remote_copy(
@@ -520,6 +528,7 @@
             vmem((TABLE, 2, 128), F32),
             vmem((64, PAR), I32),
             vmem((2, 256, 128), F32),
+            vmem((TABLE, 128), F32),
             vmem((TABLE, 128), F32),
             vmem((TABLE, 128), F32),
             vmem((3, 2, PAR, 128), F32),

time: 22 us -> 21.8 us (level)
  Pallas kernels: 21.3 us -> 21 us
    pallas_call x1, Pallas kernels: 21.3 us -> 21 us  [on_device(): pl.pallas_call(body, out_shape=vmem((LEAF, 2, 128), F32), in_specs=[hbm_s...]
where the time goes in v6:
time: 21.8 us; the launch traced here: 21.7 us
  Pallas kernels  21 us (96%)
  local copies, waits for them, and re-layouts  0.62 us (3%)
    pallas_call x1, Pallas kernels, on_device(): pl.pallas_call(body, out_shape=vmem((LEAF, 2, 128), F32), in_specs=[hbm_s...  21 us
    unnamed x1, local copies, waits for them, and re-layouts  0.62 us

profile of v6, /device:TPU:25, one launch (start us, length us, event | category | flops | bytes accessed | tf_op | source)
XLA Modules:
  0.0 21.7 jit_solution(3789336369488580443)
XLA Ops:
  0.0 21.0 %far_and_near.1 = f32[32,2,128]{2,1,0:T(2,128)S(1)} custom-call(f32[32,2,128]{2,1,0:T(2,128)} %cur.1, bf16[32,6,2,128,128]{4,3,2,1,0:T(8,128)(2,1)} %blocks.1, s32[6,32]{1,0:T(8,128)} %bitcast.3, f32[2,128,256]{2,1,0:T(8,128)} %rad.1, f32[256,1024]{1,0:T(8,128)} %itp.1, f32[8,1024]{1,0:T(8,128)} %phase.1, s32[1,256]{1,0:T(1,128)} %pmap.1, s32[1,256]{1,0:T(1,128)} %octant.1, ...), custom_call_target="tpu_custom_call" | custom-call | tf_op jit(solution)/shard_map/far_and_near/pallas_call | solution.py:512
  21.0 0.6 %copy.13 = f32[32,2,128]{2,1,0:T(2,128)} copy(f32[32,2,128]{2,1,0:T(2,128)S(1)} %far_and_near.1) | data formatting | bytes 65536

commit v7 on v6

--- a/solution.py
+++ b/solution.py
@@ -167,6 +167,8 @@
     has_after, has_before = device < CLU * SMP - 1, device > 0
     has_up, has_down = clu < CLU - 1, clu > 0
 
+    load_cur = pltpu.make_async_copy(cur, cur_v, load_sem.at[0])
+    load_cur.start()
     barrier = pltpu.get_barrier_semaphore()
 
     def greet(where):
@@ -191,7 +193,6 @@
 
     columns = pl.ds(pl.multiple_of(me * 128, 128), 128)
     loads = [
-        (cur, cur_v),
         (itp.at[:, columns], itp_v),
         (phase.at[:, columns], ph_v),
         (rad, rad_v),
@@ -203,11 +204,11 @@
         (trans.at[pl.ds(KINDS - 192, 192)], tr_v.at[pl.ds(0, 192)]),
         (trans.at[pl.ds(0, 192)], tr_v.at[pl.ds(192, 192)]),
     ]
-    copies = [
+    copies = [load_cur] + [
         pltpu.make_async_copy(source, target, load_sem.at[i])
-        for i, (source, target) in enumerate(loads)
-    ]
-    for copy in copies:
+        for i, (source, target) in enumerate(loads, 1)
+    ]
+    for copy in copies[1:]:
         copy.start()
     blk_copies = [
         pltpu.make_async_copy(
@@ -218,7 +219,7 @@
     for copy in blk_copies:
         copy.start()
 
-    copies[0].wait()
+    load_cur.wait()
     own_cur = [cur_v[:, c, :] for c in range(2)]
     for c in range(2):
         near_cur[1, c] = own_cur[c].astype(BF16)

time: 21.8 us -> 21.8 us (level)
  no operation moved by 1% of the time
where the time goes in v7:
time: 21.8 us; the launch traced here: 21.7 us
  Pallas kernels  21 us (96%)
  local copies, waits for them, and re-layouts  0.62 us (3%)
    pallas_call x1, Pallas kernels, on_device(): pl.pallas_call(body, out_shape=vmem((LEAF, 2, 128), F32), in_specs=[hbm_s...  21 us
    unnamed x1, local copies, waits for them, and re-layouts  0.62 us

profile of v7, /device:TPU:25, one launch (start us, length us, event | category | flops | bytes accessed | tf_op | source)
XLA Modules:
  0.0 21.7 jit_solution(8951694771413641438)
XLA Ops:
  0.0 21.0 %far_and_near.1 = f32[32,2,128]{2,1,0:T(2,128)S(1)} custom-call(f32[32,2,128]{2,1,0:T(2,128)} %cur.1, bf16[32,6,2,128,128]{4,3,2,1,0:T(8,128)(2,1)} %blocks.1, s32[6,32]{1,0:T(8,128)} %bitcast.3, f32[2,128,256]{2,1,0:T(8,128)} %rad.1, f32[256,1024]{1,0:T(8,128)} %itp.1, f32[8,1024]{1,0:T(8,128)} %phase.1, s32[1,256]{1,0:T(1,128)} %pmap.1, s32[1,256]{1,0:T(1,128)} %octant.1, ...), custom_call_target="tpu_custom_call" | custom-call | tf_op jit(solution)/shard_map/far_and_near/pallas_call | solution.py:513
  21.0 0.6 %copy.13 = f32[32,2,128]{2,1,0:T(2,128)} copy(f32[32,2,128]{2,1,0:T(2,128)S(1)} %far_and_near.1) | data formatting | bytes 65536
